TPU v7x, 128 devices: a whole 4x4x4 slice. The times are simulated.
128 devices in a mesh: section: 4 (over x), group: 32 (over y, z, core).
Axes of the slice: x: 4, y: 4, z: 4, core: 2. Of those that a mesh axis runs over, the one named last changes fastest.
Arguments:
- hidden: bfloat16 [2048, 8, 1024], P('group', None, 'section'), may hold values from -6 to 6
- pre_weight: bfloat16 [7, 1024, 512], replicated, may hold values from -0.0625 to 0.0625
- up1_weight: bfloat16 [16, 512, 256], replicated, may hold values from -0.1875 to 0.1875
- up2_weight: bfloat16 [16, 256, 128], replicated, may hold values from -0.25 to 0.25
- up3_weight: bfloat16 [4, 128, 64], replicated, may hold values from -0.375 to 0.375
- res3_weight: bfloat16 [3, 64, 64], replicated, may hold values from -0.4375 to 0.4375
- up4_weight: bfloat16 [4, 64, 32], replicated, may hold values from -0.5 to 0.5
- res4_weight: bfloat16 [3, 32, 32], replicated, may hold values from -0.625 to 0.625
- post_weight: bfloat16 [7, 32], replicated, may hold values from -0.375 to 0.375
- owner_device: int32 [2048, 1], replicated, may hold values from 0 to 31; in each aligned block of 16 rows (0 to 15, 16 to 31, ...) at most 2 rows name the same one
- stream_slot: int32 [2048], replicated, may hold values from 0 to 3
- start_frame: int32 [2048], replicated, may hold values from 0 to 56
- lead_frames: int32 [2048], replicated, may hold values from 1 to 4
- tail_frames: int32 [2048], replicated, may hold values from 1 to 4
Outputs:
- waveform: float32 [128, 4, 16384], P('group', 'section')
Inputs may be any that keep to these rules, and one draw needn't show every extreme that they name: `owner_device`: in each aligned block of 16 groups (the groups of one device), no owner is named by more than 2 groups, a bound that some block reaches.
All inputs are finite; a program needn't handle non-finite values.
Results may differ from a plain program's by a relative error of at most 0.015.
Values may be sent and summed in bfloat16 or wider, within the bound.
No kernel may reach another device: no remote copies, remote signals or barrier semaphores. Data moves between devices by JAX's collectives and lax.ppermute only.
A program may use at most 128 MiB of HBM per device.

v0:
```python
import jax
import jax.numpy as jnp
from jax import lax
from jax.experimental import pallas as pl
from jax.experimental.pallas import tpu as pltpu
from jax.sharding import PartitionSpec as P

CD = 16
FR = 8
SECT = 4
LANES = 32
HOP = 256
SUPER = 256
ROWS = SUPER * CD
BF = jnp.bfloat16
F32 = jnp.float32


def dot(a, b):
    return jnp.dot(a, b, preferred_element_type=F32)


def leaky(v, slope):
    return jnp.maximum(v, slope * v)


def iota(shape, dim):
    return lax.broadcasted_iota(jnp.int32, shape, dim)


def as_bf(mask):
    return jnp.where(mask, 1.0, 0.0).astype(BF)


def spread(flat, width):
    place = as_bf(iota((width, 256), 1) % width == iota((width, 256), 0))
    return dot(flat, place)


def spread_t(ref, width):
    place = as_bf(iota((width, 256), 1) % width == iota((width, 256), 0))
    return jnp.concatenate(
        [
            lax.dot_general(ref[j], place, (((0,), (0,)), ((), ())), preferred_element_type=F32)
            for j in range(ref.shape[0])
        ],
        axis=0,
    )


def blocks(rep, rows, width, entries):
    block_of = iota((rows, 256), 1) // width
    out = []
    for entry in entries:
        acc = jnp.zeros((rows, 256), F32)
        for q, j in entry:
            acc = jnp.where(block_of == q, rep[j * rows : (j + 1) * rows], acc)
        out.append(acc)
    return jnp.concatenate(out, axis=0).astype(BF)


def up_entries(places, phases):
    return [[(q, q + 1 - 2 * a) for q in range(phases) if 0 <= q + 1 - 2 * a <= 3] for a in places]


def res_entries(places, phases):
    return [
        [(q, (a - q) // 3 + 1) for q in range(phases) if a - q in (-3, 0, 3)] for a in places
    ]


def prepare(*refs):
    sources, (w2p, b3, r3, b4, r4, wc, disp, plac, win), held = refs[:11], refs[11:20], refs[20:31]
    scr, sems = refs[31:]
    copies = [pltpu.make_async_copy(a, b, sems.at[i]) for i, (a, b) in enumerate(zip(sources, held))]
    for copy in copies:
        copy.start()
    for copy in copies:
        copy.wait()
    up2, up3, res3, up4, res4, post, owners, slot, start, lead, tail = held
    section = lax.axis_index("section")
    lane = lax.axis_index("group")
    for j in range(8):
        w2p[j, :, 0:128] = up2[2 * j]
        w2p[j, :, 128:256] = up2[2 * j + 1]
    b3[...] = blocks(spread_t(up3, 64), 128, 64, up_entries((0, 1, 2, -1), 4))
    r3[...] = blocks(
        spread(res3[...].reshape(192, 64), 64), 64, 64, res_entries((*range(4), *range(-4, 0), *range(4, 8)), 4)
    )
    b4[...] = blocks(
        spread_t(up4, 32), 64, 32, up_entries((*range(4), 4, 5, -2, -1), 8)
    )
    r4[...] = blocks(
        spread(res4[...].reshape(96, 32), 32), 32, 32, res_entries((*range(8), *range(8, 12), *range(-4, 0)), 8)
    )
    scr[...] = jnp.zeros_like(scr)
    scr[0:7, 0:32] = post[...].astype(F32)
    post_t = jnp.transpose(scr[...])[0:32].astype(BF)
    tap, off = iota((128, 128), 0), iota((128, 128), 1)
    base = jnp.concatenate(
        [dot(post_t, as_bf((tap == a + 6 - off) & (tap < 7))) for a in range(8)], axis=0
    ).astype(BF)
    off, smp = iota((128, 256), 0), iota((128, 256), 1)
    for i in range(34):
        wc[i] = dot(base, as_bf((smp == 8 * (i - 1) - 3 + off) & (off < 14))).astype(BF)
    owner = jnp.concatenate([owners[:, i * 128 : (i + 1) * 128] for i in range(16)], axis=0)
    mine = jnp.where(iota((16, 128), 0) == lane // 2, 1, 0)
    spot = lane % 2 * 64 + section * CD
    rowsel = lambda v: jnp.sum(v * mine, axis=0, keepdims=True).astype(F32)
    pick = iota((128, 128), 1) == spot + iota((128, 128), 0) % CD
    column = lambda v: jnp.sum(jnp.where(pick, rowsel(v), 0.0), axis=1, keepdims=True)
    owner_col = column(owner)
    owner_row = jnp.sum(
        jnp.where(iota((128, 128), 0) == iota((128, 128), 1), owner_col, 0.0), axis=0, keepdims=True
    )
    before = (owner_col[0:CD] == owner_row) & (iota((CD, 128), 0) < iota((CD, 128), 1) % CD)
    rank = jnp.sum(jnp.where(before, 1.0, 0.0), axis=0, keepdims=True)
    dest = (2.0 * owner_row + rank).astype(jnp.int32)
    r_d, l_d = iota((512, 128), 0), iota((512, 128), 1)
    disp[...] = as_bf((r_d // FR == dest) & (r_d % FR == l_d // CD))
    t = ((iota((128, 256), 0) // CD) * HOP + iota((128, 256), 1)).astype(F32) + 0.5
    win[...] = jnp.minimum(1.0, t / (HOP * column(lead[...]))) * jnp.minimum(
        1.0, (FR * HOP - t) / (HOP * column(tail[...]))
    )
    l_g = iota((16, 128), 1)
    owned = jnp.where((l_g // CD % SECT == section) & (owner == lane), 1.0, 0.0)
    r_l, c_l = iota((128, 128), 0), iota((128, 128), 1)
    order = dot(owned.astype(BF), as_bf((r_l < c_l) & (r_l // 64 == c_l // 64)))
    target = (slot[...] * 64 + start[...]).astype(F32) * owned
    l_p = iota((16, 512), 1)
    item = jnp.zeros((16, 512), F32)
    for half in range(2):
        for c in range(2):
            at = jnp.sum(
                jnp.where((order == float(c)) & (l_g // 64 == half), target, 0.0), axis=1, keepdims=True
            )
            item = jnp.where(l_p // FR % 4 == 2 * half + c, at, item)
    item = jnp.where(l_p // 32 == iota((16, 512), 0), item, 0.0)
    goal = jnp.sum(item, axis=0, keepdims=True).astype(jnp.int32) + iota((1, 512), 1) % FR
    plac[...] = as_bf(iota((256, 512), 0) == goal)


def edges(ref, first, rows):
    return jnp.concatenate(
        [ref[pl.ds(first + 2 * CD, rows), 0:128], ref[pl.ds(first, rows), 128:256]], axis=1
    )


CHUNK = 512


def synthesize(
    hid, rec1, rec2, rec3, pre, up1_hbm, w2p, b3, r3, b4, r4, wc, disp, win, out,
    up1, xb, a0, a1, a2, u3, i3, a3, sem,
):
    section = lax.axis_index("section")
    u4, i4, a4 = u3, i3, a2
    fetch = pltpu.make_async_copy(up1_hbm, up1, sem)
    fetch.start()
    for ref, pad in ((xb, 3), (a0, 1), (a1, 1), (a2, 1), (i3, 1), (a3, 1)):
        width = ref.shape[-1]
        zero = jnp.zeros((pad * CD, width), BF)
        ref[0 : pad * CD, :] = zero
        ref[ref.shape[0] - pad * CD :, :] = zero

    r, c = iota((128, 128), 0), iota((128, 128), 1)
    turn = as_bf(c == (r % CD) * FR + r // CD)
    own = hid[pl.ds(pl.multiple_of(section * 128, 128), 128), :]
    for d, block in enumerate((own, rec1[...], rec2[...], rec3[...])):
        xb[3 * CD : 3 * CD + 128, d * 256 : (d + 1) * 256] = dot(turn, block).astype(BF)
    acc = jnp.zeros((128, 512), F32)
    for d in range(SECT):
        rows = pl.ds(pl.multiple_of(lax.rem(section + SECT - d, SECT) * 256, 256), 256)
        for j in range(7):
            acc = acc + dot(xb[j * CD : j * CD + 128, d * 256 : (d + 1) * 256], pre[j, rows, :])
    a0[CD : CD + 128, :] = leaky(acc, 0.1).astype(BF)

    fetch.wait()
    for p in range(8):
        shift, j = (0, p + 12) if p < 4 else (2 * CD, p - 4)
        y = dot(a0[CD : CD + 128, :], up1[p + 4]) + dot(a0[shift : shift + 128, :], up1[j])
        y = leaky(y, 0.1).astype(BF)
        for i in range(FR):
            at = (8 * i + p + 1) * CD
            a1[at : at + CD, :] = y[i * CD : (i + 1) * CD]

    for part in range(4):
        first = part * 256
        here = a1[first + CD : first + CD + 256, :]
        earlier = a1[first : first + 256, :]
        later = a1[first + 2 * CD : first + 2 * CD + 256, :]
        for q in range(4):
            side, j = (earlier, q + 6) if q < 2 else (later, q - 2)
            y = leaky(dot(here, w2p[q + 2]) + dot(side, w2p[j]), 0.1).astype(BF)
            for i in range(16):
                at = (4 * (part * 16 + i) + q + 1) * CD
                a2[at : at + CD, :] = y[i * CD : (i + 1) * CD]

    def each(body):
        @pl.loop(0, ROWS // CHUNK)
        def _(n):
            body(pl.multiple_of(n * CHUNK, CHUNK))

    @each
    def _(first):
        y = dot(a2[pl.ds(first + CD, CHUNK), :], b3[0:256, :])
        y = y + dot(edges(a2, first, CHUNK), b3[256:512, :])
        u3[pl.ds(first, CHUNK), :] = y
        i3[pl.ds(first + CD, CHUNK), :] = leaky(y, 0.1).astype(BF)

    @each
    def _(first):
        y = u3[pl.ds(first, CHUNK), :] + dot(i3[pl.ds(first + CD, CHUNK), :], r3[0:256, :])
        y = y + dot(i3[pl.ds(first, CHUNK), :], r3[256:512, :])
        y = y + dot(i3[pl.ds(first + 2 * CD, CHUNK), :], r3[512:768, :])
        a3[pl.ds(first + CD, CHUNK), :] = leaky(y, 0.1).astype(BF)

    @each
    def _(first):
        y = dot(a3[pl.ds(first + CD, CHUNK), :], b4[0:256, :])
        y = y + dot(edges(a3, first, CHUNK), b4[256:512, :])
        u4[pl.ds(first, CHUNK), :] = y
        i4[pl.ds(first + CD, CHUNK), :] = leaky(y, 0.1).astype(BF)

    @each
    def _(first):
        y = u4[pl.ds(first, CHUNK), :] + dot(i4[pl.ds(first + CD, CHUNK), :], r4[0:256, :])
        y = y + dot(edges(i4, first, CHUNK), r4[256:512, :])
        a4[pl.ds(first + CD, CHUNK), :] = leaky(y, 0.01).astype(BF)

    acc = jnp.zeros((128, 256), F32)
    for i in range(34):
        rows = [a4[fr * 512 + i * CD : fr * 512 + (i + 1) * CD, :] for fr in range(FR)]
        acc = acc + dot(jnp.concatenate(rows, axis=0), wc[i])
    wave = (jnp.tanh(acc) * win[...]).astype(BF)
    out[...] = dot(disp[...], wave).astype(BF)


def place(plac, rec, out):
    y = dot(plac[...], rec[...])
    out[pl.ds(0, 256, stride=2), :] = y[:, 0:128]
    out[pl.ds(1, 256, stride=2), :] = y[:, 128:256]


VM = pl.BlockSpec(memory_space=pltpu.VMEM)
HB = pl.BlockSpec(memory_space=pltpu.HBM)
LIMIT = 24 * 1024 * 1024


def shards(
    hidden, pre_weight, up1_weight, up2_weight, up3_weight, res3_weight, up4_weight, res4_weight,
    post_weight, owner_device, stream_slot, start_frame, lead_frames, tail_frames,
):
    section = lax.axis_index("section")
    rows_here = hidden.reshape(SECT, 128, 256)
    received = []
    for d in (1, 2, 3):
        block = lax.dynamic_index_in_dim(rows_here, (section + d) % SECT, 0, keepdims=False)
        received.append(lax.ppermute(block, "section", [(i, (i + d) % SECT) for i in range(SECT)]))
    shape = jax.ShapeDtypeStruct
    prepared = pl.pallas_call(
        prepare,
        out_shape=(
            shape((8, 256, 256), BF),
            shape((512, 256), BF),
            shape((768, 256), BF),
            shape((512, 256), BF),
            shape((512, 256), BF),
            shape((34, 256, 256), BF),
            shape((512, 128), BF),
            shape((256, 512), BF),
            shape((128, 256), F32),
        ),
        in_specs=[HB] * 11,
        out_specs=(VM,) * 9,
        scratch_shapes=[
            pltpu.VMEM((16, 256, 128), BF),
            pltpu.VMEM((4, 64, 128), BF),
            pltpu.VMEM((3, 64, 64), BF),
            pltpu.VMEM((4, 32, 64), BF),
            pltpu.VMEM((3, 32, 32), BF),
            pltpu.VMEM((7, 32), BF),
            pltpu.VMEM((1, 2048), jnp.int32),
            *[pltpu.VMEM((16, 128), jnp.int32)] * 4,
            pltpu.VMEM((128, 128), F32),
            pltpu.SemaphoreType.DMA((11,)),
        ],
        compiler_params=pltpu.CompilerParams(vmem_limit_bytes=16 * 1024 * 1024),
        cost_estimate=pl.CostEstimate(flops=2_000_000_000, bytes_accessed=8_000_000, transcendentals=0),
        name="prepare",
    )(
        *(
            pltpu.with_memory_space_constraint(v, pltpu.HBM)
            for v in (
                up2_weight, jnp.swapaxes(up3_weight, 1, 2), res3_weight, jnp.swapaxes(up4_weight, 1, 2),
                res4_weight, post_weight, owner_device.reshape(1, 2048),
                *(v.reshape(16, 128) for v in (stream_slot, start_frame, lead_frames, tail_frames)),
            )
        )
    )
    w2p, b3, r3, b4, r4, wc, disp, plac, win = prepared
    sent = pl.pallas_call(
        synthesize,
        out_shape=shape((512, 256), BF),
        in_specs=[VM] * 5 + [HB] + [VM] * 8,
        out_specs=VM,
        scratch_shapes=[
            pltpu.VMEM((16, 512, 256), BF),
            pltpu.VMEM((128 + 6 * CD, 1024), BF),
            pltpu.VMEM((128 + 2 * CD, 512), BF),
            pltpu.VMEM((1024 + 2 * CD, 256), BF),
            pltpu.VMEM((ROWS + 2 * CD, 256), BF),
            pltpu.VMEM((ROWS, 256), F32),
            pltpu.VMEM((ROWS + 2 * CD, 256), BF),
            pltpu.VMEM((ROWS + 2 * CD, 256), BF),
            pltpu.SemaphoreType.DMA,
        ],
        compiler_params=pltpu.CompilerParams(vmem_limit_bytes=LIMIT),
        cost_estimate=pl.CostEstimate(
            flops=8_000_000_000, bytes_accessed=20_000_000, transcendentals=32768
        ),
        name="synthesize",
    )(hidden.reshape(512, 256), *received, pre_weight, pltpu.with_memory_space_constraint(up1_weight, pltpu.HBM), w2p, b3, r3, b4, r4, wc, disp, win)
    waves = lax.all_to_all(sent, "group", split_axis=0, concat_axis=0, tiled=True)
    streams = pl.pallas_call(
        place,
        out_shape=shape((512, 128), F32),
        in_specs=[VM] * 2,
        out_specs=VM,
        compiler_params=pltpu.CompilerParams(vmem_limit_bytes=8 * 1024 * 1024),
        name="place",
    )(plac, waves)
    return streams.reshape(4, 1, 64 * HOP)


def solution(mesh):
    in_specs = (P("group", None, "section"),) + (P(),) * 13
    return jax.shard_map(
        shards, mesh=mesh, in_specs=in_specs, out_specs=P("group", "section", None), check_vma=False
    )
```

profile of v0, /device:TPU:1, one launch (start us, length us, event | category | flops | bytes accessed | tf_op | source)
XLA Modules:
  0.0 45.8 jit_solution(10949443205117310795)
XLA Ops:
  0.0 0.0 copy-start
  0.0 0.0 copy-start.1
  0.0 1.1 %dynamic-slice_bitcast_fusion = (bf16[128,256]{1,0:T(8,128)(2,1)S(1)}, bf16[128,256]{1,0:T(8,128)(2,1)S(1)}, bf16[128,256]{1,0:T(8,128)(2,1)S(1)}) fusion(bf16[4,128,256]{2,1,0:T(8,128)(2,1)} %bitcast.20, s32[]{:T(128)S(6)} %select_n.30, s32[]{:T(128)S(6)} %select_n.28, s32[]{:T(128)S(6)} %select_n.26), kind=kLoop, calls=%fused_computation | loop fusion | bytes 393228 | tf_op jit(solution)/shard_map/jit(dynamic_index_in_dim)/squeeze | solution.py:258
  1.1 3.4 %collective-permute-start.2 = (bf16[128,256]{1,0:T(8,128)(2,1)S(1)}, bf16[128,256]{1,0:T(8,128)(2,1)S(1)}, u32[]{:S(2)}, u32[]{:S(2)}) collective-permute-start(bf16[128,256]{1,0:T(8,128)(2,1)S(1)} %get-tuple-element.23), channel_id=1, source_target_pairs={{0,96},{32,0},{64,32},{96,64},{1,97},{33,1},{65,33},{97,65},{2,98}... | collective-permute-start | bytes 196616 | tf_op jit(solution)/shard_map/ppermute | solution.py:259
  4.5 0.5 %collective-permute-start.1 = (bf16[128,256]{1,0:T(8,128)(2,1)S(1)}, bf16[128,256]{1,0:T(8,128)(2,1)S(1)}, u32[]{:S(2)}, u32[]{:S(2)}) collective-permute-start(bf16[128,256]{1,0:T(8,128)(2,1)S(1)} %get-tuple-element.24), channel_id=1, source_target_pairs={{0,64},{32,96},{64,0},{96,32},{1,65},{33,97},{65,1},{97,33},{2,66}... | collective-permute-start | bytes 196616 | tf_op jit(solution)/shard_map/ppermute | solution.py:259
  5.0 0.6 %collective-permute-start = (bf16[128,256]{1,0:T(8,128)(2,1)S(1)}, bf16[128,256]{1,0:T(8,128)(2,1)S(1)}, u32[]{:S(2)}, u32[]{:S(2)}) collective-permute-start(bf16[128,256]{1,0:T(8,128)(2,1)S(1)} %get-tuple-element.25), channel_id=1, source_target_pairs={{0,32},{32,64},{64,96},{96,0},{1,33},{33,65},{65,97},{97,1},{2,34}... | collective-permute-start | bytes 196616 | tf_op jit(solution)/shard_map/ppermute | solution.py:259
  5.6 3.1 %prepare.1 = (bf16[8,256,256]{2,1,0:T(8,128)(2,1)S(1)}, bf16[512,256]{1,0:T(8,128)(2,1)S(1)}, bf16[768,256]{1,0:T(8,128)(2,1)S(1)}, bf16[512,256]{1,0:T(8,128)(2...) custom-call(bf16[16,256,128]{2,1,0:T(8,128)(2,1)} %refs_0_.1, ...), custom_call_target="tpu_custom_call" | custom-call | flops 2000000000 | bytes 8000000 | tf_op jit(solution)/shard_map/prepare/pallas_call | solution.py:261
  8.7 0.0 collective-permute-done.2.rec3
  8.7 0.4 collective-permute-done.1.rec2
  9.1 0.7 %collective-permute-done.rec1 = bf16[128,256]{1,0:T(8,128)(2,1)S(1)} collective-permute-done((bf16[128,256]{1,0:T(8,128)(2,1)S(1)}, bf16[128,256]{1,0:T(8,128)(2,1)S(1)}, u32[]{:S(2)}, u32[]{:S(2)}) %collective-permute-start) | collective-permute-done | bytes 65568 | tf_op jit(solution)/shard_map/ppermute | solution.py:259
  9.8 0.0 copy-done
  9.8 0.0 copy-done.1
  9.8 16.1 %synthesize.1 = bf16[512,256]{1,0:T(8,128)(2,1)S(1)} custom-call(bf16[512,256]{1,0:T(8,128)(2,1)S(1)} %bitcast.21, bf16[128,256]{1,0:T(8,128)(2,1)S(1)} %collective-permute-done.rec1, bf16[128,256]{1,0:T(8,128)(2,1)S(1)} %collective-permute-done.1.rec2, bf16[128,256]{1,0:T(8,128)(2,1)S(1)} %collective-permute-done.2.rec3, ...), custom_call_target="tpu_custom_call" | custom-call | flops 8000000000 | bytes 20000000 | tf_op jit(solution)/shard_map/synthesize/pallas_call | solution.py:302
  25.9 19.0 %all_to_all.11 = bf16[32,16,256]{2,1,0:T(8,128)(2,1)S(1)} all-to-all(bf16[32,16,256]{2,1,0:T(8,128)(2,1)S(1)} %bitcast.19), channel_id=1, replica_groups=mesh['section'=4,'group'=32] {'group'}, dimensions={0} | all-to-all | bytes 524288 | tf_op jit(solution)/shard_map/all_to_all | solution.py:324
  44.9 0.9 %place.1 = f32[512,128]{1,0:T(8,128)} custom-call(bf16[256,512]{1,0:T(8,128)(2,1)S(1)} %get-tuple-element.14.plac, bf16[512,256]{1,0:T(8,128)(2,1)S(1)} %bitcast.18), custom_call_target="tpu_custom_call" | custom-call | tf_op jit(solution)/shard_map/place/pallas_call | solution.py:325
Async XLA Ops:
  0.0 9.8 %copy-start = (bf16[64,8,256]{2,1,0:T(8,128)(2,1)S(1)}, bf16[64,8,256]{2,1,0:T(8,128)(2,1)}, u32[]{:S(2)}) copy-start(bf16[64,8,256]{2,1,0:T(8,128)(2,1)} %param.14) | copy-start | bytes 786436
  0.0 9.8 %copy-start.1 = (bf16[7,1024,512]{2,1,0:T(8,128)(2,1)S(1)}, bf16[7,1024,512]{2,1,0:T(8,128)(2,1)}, u32[]{:S(2)}) copy-start(bf16[7,1024,512]{2,1,0:T(8,128)(2,1)} %pre.1) | copy-start | bytes 22020100
  1.1 7.6 %collective-permute-start.2 = (bf16[128,256]{1,0:T(8,128)(2,1)S(1)}, bf16[128,256]{1,0:T(8,128)(2,1)S(1)}, u32[]{:S(2)}, u32[]{:S(2)}) collective-permute-start(bf16[128,256]{1,0:T(8,128)(2,1)S(1)} %get-tuple-element.23), channel_id=1, source_target_pairs={{0,96},{32,0},{64,32},{96,64},{1,97},{33,1},{65,33},{97,65},{2,98}... | collective-permute-start | bytes 196616 | tf_op jit(solution)/shard_map/ppermute | solution.py:259
  4.5 4.7 %collective-permute-start.1 = (bf16[128,256]{1,0:T(8,128)(2,1)S(1)}, bf16[128,256]{1,0:T(8,128)(2,1)S(1)}, u32[]{:S(2)}, u32[]{:S(2)}) collective-permute-start(bf16[128,256]{1,0:T(8,128)(2,1)S(1)} %get-tuple-element.24), channel_id=1, source_target_pairs={{0,64},{32,96},{64,0},{96,32},{1,65},{33,97},{65,1},{97,33},{2,66}... | collective-permute-start | bytes 196616 | tf_op jit(solution)/shard_map/ppermute | solution.py:259
  5.0 4.8 %collective-permute-start = (bf16[128,256]{1,0:T(8,128)(2,1)S(1)}, bf16[128,256]{1,0:T(8,128)(2,1)S(1)}, u32[]{:S(2)}, u32[]{:S(2)}) collective-permute-start(bf16[128,256]{1,0:T(8,128)(2,1)S(1)} %get-tuple-element.25), channel_id=1, source_target_pairs={{0,32},{32,64},{64,96},{96,0},{1,33},{33,65},{65,97},{97,1},{2,34}... | collective-permute-start | bytes 196616 | tf_op jit(solution)/shard_map/ppermute | solution.py:259
where the time goes:
time: 46 us; the launch traced here: 45.8 us
  Pallas kernels  20.1 us (44%)
  blocking collectives  19 us (41%)
  starting transfers between devices  4.5 us (10%)
  local copies, waits for them, and re-layouts  1.07 us (2%)
  waiting for transfers between devices  1.06 us (2%)
    all_to_all x1, blocking collectives, shards(): lax.all_to_all(sent, 'group', split_axis=0, concat_axis=0, tiled=True)  19 us
    pallas_call x1, Pallas kernels, shards(): pl.pallas_call(synthesize, out_shape=shape((512, 256), BF), in_specs=[VM]...  16.1 us
    ppermute x3, starting transfers between devices, shards(): lax.ppermute(block, 'section', [(i, (i + d) % SECT) for i in range(SECT)])  4.5 us
    pallas_call x1, Pallas kernels, shards(): pl.pallas_call(prepare, out_shape=(shape((8, 256, 256), BF), shape((512,...  3.12 us
    squeeze x1, local copies, waits for them, and re-layouts, shards(): lax.dynamic_index_in_dim(rows_here, (section + d) % SECT, 0, keepdims=False)  1.07 us
    ppermute x3, waiting for transfers between devices, shards(): lax.ppermute(block, 'section', [(i, (i + d) % SECT) for i in range(SECT)])  1.06 us
    pallas_call x1, Pallas kernels, shards(): pl.pallas_call(place, out_shape=shape((512, 128), F32), in_specs=[VM] * 2...  0.94 us
  transfers between devices with their start and end apart: 3, of which 2 were waited for; matrix products, arithmetic and copies ran while one was open for 0% of the time, Pallas kernels for 7%

commit v1 on v0

--- a/solution.py
+++ b/solution.py
@@ -70,12 +70,12 @@
 
 
 def prepare(*refs):
-    sources, (w2p, b3, r3, b4, r4, wc, disp, plac, win), held = refs[:11], refs[11:20], refs[20:31]
-    scr, sems = refs[31:]
-    copies = [pltpu.make_async_copy(a, b, sems.at[i]) for i, (a, b) in enumerate(zip(sources, held))]
+    sources, (up1, w2p, b3, r3, b4, r4, wc, disp, plac, win), held = refs[:12], refs[12:22], refs[22:33]
+    scr, sems = refs[33:]
+    copies = [pltpu.make_async_copy(a, b, sems.at[i]) for i, (a, b) in enumerate(zip(sources, (*held, up1)))]
     for copy in copies:
         copy.start()
-    for copy in copies:
+    for copy in copies[:11]:
         copy.wait()
     up2, up3, res3, up4, res4, post, owners, slot, start, lead, tail = held
     section = lax.axis_index("section")
@@ -138,11 +138,12 @@
     item = jnp.where(l_p // 32 == iota((16, 512), 0), item, 0.0)
     goal = jnp.sum(item, axis=0, keepdims=True).astype(jnp.int32) + iota((1, 512), 1) % FR
     plac[...] = as_bf(iota((256, 512), 0) == goal)
+    copies[11].wait()
 
 
 def edges(ref, first, rows):
     return jnp.concatenate(
-        [ref[pl.ds(first + 2 * CD, rows), 0:128], ref[pl.ds(first, rows), 128:256]], axis=1
+        [ref[first + 2 * CD : first + 2 * CD + rows, 0:128], ref[first : first + rows, 128:256]], axis=1
     )
 
 
@@ -150,14 +151,11 @@
 
 
 def synthesize(
-    hid, rec1, rec2, rec3, pre, up1_hbm, w2p, b3, r3, b4, r4, wc, disp, win, out,
-    up1, xb, a0, a1, a2, u3, i3, a3, sem,
+    hid, rec1, rec2, rec3, pre, up1, w2p, b3, r3, b4, r4, wc, disp, win, out,
+    xb, a0, a1, a2, u3, i3, a3, u4, i4, a4,
 ):
     section = lax.axis_index("section")
-    u4, i4, a4 = u3, i3, a2
-    fetch = pltpu.make_async_copy(up1_hbm, up1, sem)
-    fetch.start()
-    for ref, pad in ((xb, 3), (a0, 1), (a1, 1), (a2, 1), (i3, 1), (a3, 1)):
+    for ref, pad in ((xb, 3), (a0, 1), (a1, 1), (a2, 1), (i3, 1), (a3, 1), (i4, 1), (a4, 1)):
         width = ref.shape[-1]
         zero = jnp.zeros((pad * CD, width), BF)
         ref[0 : pad * CD, :] = zero
@@ -175,7 +173,6 @@
             acc = acc + dot(xb[j * CD : j * CD + 128, d * 256 : (d + 1) * 256], pre[j, rows, :])
     a0[CD : CD + 128, :] = leaky(acc, 0.1).astype(BF)
 
-    fetch.wait()
     for p in range(8):
         shift, j = (0, p + 12) if p < 4 else (2 * CD, p - 4)
         y = dot(a0[CD : CD + 128, :], up1[p + 4]) + dot(a0[shift : shift + 128, :], up1[j])
@@ -196,37 +193,39 @@
                 at = (4 * (part * 16 + i) + q + 1) * CD
                 a2[at : at + CD, :] = y[i * CD : (i + 1) * CD]
 
-    def each(body):
-        @pl.loop(0, ROWS // CHUNK)
-        def _(n):
-            body(pl.multiple_of(n * CHUNK, CHUNK))
-
-    @each
-    def _(first):
-        y = dot(a2[pl.ds(first + CD, CHUNK), :], b3[0:256, :])
-        y = y + dot(edges(a2, first, CHUNK), b3[256:512, :])
-        u3[pl.ds(first, CHUNK), :] = y
-        i3[pl.ds(first + CD, CHUNK), :] = leaky(y, 0.1).astype(BF)
-
-    @each
-    def _(first):
-        y = u3[pl.ds(first, CHUNK), :] + dot(i3[pl.ds(first + CD, CHUNK), :], r3[0:256, :])
-        y = y + dot(i3[pl.ds(first, CHUNK), :], r3[256:512, :])
-        y = y + dot(i3[pl.ds(first + 2 * CD, CHUNK), :], r3[512:768, :])
-        a3[pl.ds(first + CD, CHUNK), :] = leaky(y, 0.1).astype(BF)
-
-    @each
-    def _(first):
-        y = dot(a3[pl.ds(first + CD, CHUNK), :], b4[0:256, :])
-        y = y + dot(edges(a3, first, CHUNK), b4[256:512, :])
-        u4[pl.ds(first, CHUNK), :] = y
-        i4[pl.ds(first + CD, CHUNK), :] = leaky(y, 0.1).astype(BF)
-
-    @each
-    def _(first):
-        y = u4[pl.ds(first, CHUNK), :] + dot(i4[pl.ds(first + CD, CHUNK), :], r4[0:256, :])
-        y = y + dot(edges(i4, first, CHUNK), r4[256:512, :])
-        a4[pl.ds(first + CD, CHUNK), :] = leaky(y, 0.01).astype(BF)
+    def third(lo, hi):
+        rows = hi - lo
+        y = dot(jnp.concatenate([a2[lo + CD : hi + CD, :], edges(a2, lo, rows)], axis=1), b3[...])
+        u3[lo:hi, :] = y
+        i3[lo + CD : hi + CD, :] = leaky(y, 0.1).astype(BF)
+
+    def third_res(lo, hi):
+        near = [i3[lo + CD : hi + CD, :], i3[lo:hi, :], i3[lo + 2 * CD : hi + 2 * CD, :]]
+        y = u3[lo:hi, :] + dot(jnp.concatenate(near, axis=1), r3[...])
+        a3[lo + CD : hi + CD, :] = leaky(y, 0.1).astype(BF)
+
+    def fourth(lo, hi):
+        rows = hi - lo
+        y = dot(jnp.concatenate([a3[lo + CD : hi + CD, :], edges(a3, lo, rows)], axis=1), b4[...])
+        u4[lo:hi, :] = y
+        i4[lo + CD : hi + CD, :] = leaky(y, 0.1).astype(BF)
+
+    def fourth_res(lo, hi):
+        rows = hi - lo
+        y = u4[lo:hi, :] + dot(
+            jnp.concatenate([i4[lo + CD : hi + CD, :], edges(i4, lo, rows)], axis=1), r4[...]
+        )
+        a4[lo + CD : hi + CD, :] = leaky(y, 0.01).astype(BF)
+
+    stages = (third, third_res, fourth, fourth_res)
+    chunks = ROWS // CHUNK
+    for step in range(chunks + len(stages) - 1):
+        for behind in reversed(range(len(stages))):
+            n = step - behind
+            if 0 <= n < chunks:
+                lo = max(0, n * CHUNK - behind * CD)
+                hi = ROWS if n == chunks - 1 else (n + 1) * CHUNK - behind * CD
+                stages[behind](lo, hi)
 
     acc = jnp.zeros((128, 256), F32)
     for i in range(34):
@@ -244,7 +243,7 @@
 
 VM = pl.BlockSpec(memory_space=pltpu.VMEM)
 HB = pl.BlockSpec(memory_space=pltpu.HBM)
-LIMIT = 24 * 1024 * 1024
+LIMIT = 33 * 1024 * 1024
 
 
 def shards(
@@ -261,6 +260,7 @@
     prepared = pl.pallas_call(
         prepare,
         out_shape=(
+            shape((16, 512, 256), BF),
             shape((8, 256, 256), BF),
             shape((512, 256), BF),
             shape((768, 256), BF),
@@ -271,8 +271,8 @@
             shape((256, 512), BF),
             shape((128, 256), F32),
         ),
-        in_specs=[HB] * 11,
-        out_specs=(VM,) * 9,
+        in_specs=[HB] * 12,
+        out_specs=(VM,) * 10,
         scratch_shapes=[
             pltpu.VMEM((16, 256, 128), BF),
             pltpu.VMEM((4, 64, 128), BF),
@@ -283,9 +283,9 @@
             pltpu.VMEM((1, 2048), jnp.int32),
             *[pltpu.VMEM((16, 128), jnp.int32)] * 4,
             pltpu.VMEM((128, 128), F32),
-            pltpu.SemaphoreType.DMA((11,)),
+            pltpu.SemaphoreType.DMA((12,)),
         ],
-        compiler_params=pltpu.CompilerParams(vmem_limit_bytes=16 * 1024 * 1024),
+        compiler_params=pltpu.CompilerParams(vmem_limit_bytes=14 * 1024 * 1024),
         cost_estimate=pl.CostEstimate(flops=2_000_000_000, bytes_accessed=8_000_000, transcendentals=0),
         name="prepare",
     )(
@@ -295,17 +295,17 @@
                 up2_weight, jnp.swapaxes(up3_weight, 1, 2), res3_weight, jnp.swapaxes(up4_weight, 1, 2),
                 res4_weight, post_weight, owner_device.reshape(1, 2048),
                 *(v.reshape(16, 128) for v in (stream_slot, start_frame, lead_frames, tail_frames)),
+                up1_weight,
             )
         )
     )
-    w2p, b3, r3, b4, r4, wc, disp, plac, win = prepared
+    up1, w2p, b3, r3, b4, r4, wc, disp, plac, win = prepared
     sent = pl.pallas_call(
         synthesize,
         out_shape=shape((512, 256), BF),
-        in_specs=[VM] * 5 + [HB] + [VM] * 8,
+        in_specs=[VM] * 14,
         out_specs=VM,
         scratch_shapes=[
-            pltpu.VMEM((16, 512, 256), BF),
             pltpu.VMEM((128 + 6 * CD, 1024), BF),
             pltpu.VMEM((128 + 2 * CD, 512), BF),
             pltpu.VMEM((1024 + 2 * CD, 256), BF),
@@ -313,14 +313,16 @@
             pltpu.VMEM((ROWS, 256), F32),
             pltpu.VMEM((ROWS + 2 * CD, 256), BF),
             pltpu.VMEM((ROWS + 2 * CD, 256), BF),
-            pltpu.SemaphoreType.DMA,
+            pltpu.VMEM((ROWS, 256), F32),
+            pltpu.VMEM((ROWS + 2 * CD, 256), BF),
+            pltpu.VMEM((ROWS + 2 * CD, 256), BF),
         ],
         compiler_params=pltpu.CompilerParams(vmem_limit_bytes=LIMIT),
         cost_estimate=pl.CostEstimate(
             flops=8_000_000_000, bytes_accessed=20_000_000, transcendentals=32768
         ),
         name="synthesize",
-    )(hidden.reshape(512, 256), *received, pre_weight, pltpu.with_memory_space_constraint(up1_weight, pltpu.HBM), w2p, b3, r3, b4, r4, wc, disp, win)
+    )(hidden.reshape(512, 256), *received, pre_weight, up1, w2p, b3, r3, b4, r4, wc, disp, win)
     waves = lax.all_to_all(sent, "group", split_axis=0, concat_axis=0, tiled=True)
     streams = pl.pallas_call(
         place,

time: 46 us -> 39.7 us (0.86)
  Pallas kernels: 20.1 us -> 14 us
    pallas_call x1, Pallas kernels: 16.1 us -> 9.89 us  [shards(): pl.pallas_call(synthesize, out_shape=shape((512, 256), BF), in_specs=[VM]...]
  transfers between devices with their start and end apart: 3 -> 3, of which waited for: 2 -> 2; matrix products, arithmetic and copies ran while one was open for 0% -> 0% of each run, Pallas kernels for 7% -> 8%
where the time goes in v1:
time: 39.7 us; the launch traced here: 39.6 us
  blocking collectives  19 us (48%)
  Pallas kernels  14 us (35%)
  starting transfers between devices  4.5 us (11%)
  local copies, waits for them, and re-layouts  1.07 us (3%)
  waiting for transfers between devices  1.05 us (3%)
    all_to_all x1, blocking collectives, shards(): lax.all_to_all(sent, 'group', split_axis=0, concat_axis=0, tiled=True)  19 us
    pallas_call x1, Pallas kernels, shards(): pl.pallas_call(synthesize, out_shape=shape((512, 256), BF), in_specs=[VM]...  9.89 us
    ppermute x3, starting transfers between devices, shards(): lax.ppermute(block, 'section', [(i, (i + d) % SECT) for i in range(SECT)])  4.5 us
    pallas_call x1, Pallas kernels, shards(): pl.pallas_call(prepare, out_shape=(shape((16, 512, 256), BF), shape((8, 2...  3.13 us
    squeeze x1, local copies, waits for them, and re-layouts, shards(): lax.dynamic_index_in_dim(rows_here, (section + d) % SECT, 0, keepdims=False)  1.07 us
    ppermute x3, waiting for transfers between devices, shards(): lax.ppermute(block, 'section', [(i, (i + d) % SECT) for i in range(SECT)])  1.05 us
    pallas_call x1, Pallas kernels, shards(): pl.pallas_call(place, out_shape=shape((512, 128), F32), in_specs=[VM] * 2...  0.93 us
  transfers between devices with their start and end apart: 3, of which 2 were waited for; matrix products, arithmetic and copies ran while one was open for 0% of the time, Pallas kernels for 8%

profile of v1, /device:TPU:1, one launch (start us, length us, event | category | flops | bytes accessed | tf_op | source)
XLA Modules:
  0.0 39.6 jit_solution(16895287893576395530)
XLA Ops:
  0.0 0.0 copy-start
  0.0 0.0 copy-start.1
  0.0 1.1 %dynamic-slice_bitcast_fusion = (bf16[128,256]{1,0:T(8,128)(2,1)S(1)}, bf16[128,256]{1,0:T(8,128)(2,1)S(1)}, bf16[128,256]{1,0:T(8,128)(2,1)S(1)}) fusion(bf16[4,128,256]{2,1,0:T(8,128)(2,1)} %bitcast.20, s32[]{:T(128)S(6)} %select_n.30, s32[]{:T(128)S(6)} %select_n.28, s32[]{:T(128)S(6)} %select_n.26), kind=kLoop, calls=%fused_computation | loop fusion | bytes 393228 | tf_op jit(solution)/shard_map/jit(dynamic_index_in_dim)/squeeze | solution.py:257
  1.1 3.4 %collective-permute-start.2 = (bf16[128,256]{1,0:T(8,128)(2,1)S(1)}, bf16[128,256]{1,0:T(8,128)(2,1)S(1)}, u32[]{:S(2)}, u32[]{:S(2)}) collective-permute-start(bf16[128,256]{1,0:T(8,128)(2,1)S(1)} %get-tuple-element.25), channel_id=1, source_target_pairs={{0,96},{32,0},{64,32},{96,64},{1,97},{33,1},{65,33},{97,65},{2,98}... | collective-permute-start | bytes 196616 | tf_op jit(solution)/shard_map/ppermute | solution.py:258
  4.5 0.5 %collective-permute-start.1 = (bf16[128,256]{1,0:T(8,128)(2,1)S(1)}, bf16[128,256]{1,0:T(8,128)(2,1)S(1)}, u32[]{:S(2)}, u32[]{:S(2)}) collective-permute-start(bf16[128,256]{1,0:T(8,128)(2,1)S(1)} %get-tuple-element.26), channel_id=1, source_target_pairs={{0,64},{32,96},{64,0},{96,32},{1,65},{33,97},{65,1},{97,33},{2,66}... | collective-permute-start | bytes 196616 | tf_op jit(solution)/shard_map/ppermute | solution.py:258
  5.0 0.6 %collective-permute-start = (bf16[128,256]{1,0:T(8,128)(2,1)S(1)}, bf16[128,256]{1,0:T(8,128)(2,1)S(1)}, u32[]{:S(2)}, u32[]{:S(2)}) collective-permute-start(bf16[128,256]{1,0:T(8,128)(2,1)S(1)} %get-tuple-element.27), channel_id=1, source_target_pairs={{0,32},{32,64},{64,96},{96,0},{1,33},{33,65},{65,97},{97,1},{2,34}... | collective-permute-start | bytes 196616 | tf_op jit(solution)/shard_map/ppermute | solution.py:258
  5.6 3.1 %prepare.1 = (bf16[16,512,256]{2,1,0:T(8,128)(2,1)S(1)}, bf16[8,256,256]{2,1,0:T(8,128)(2,1)S(1)}, bf16[512,256]{1,0:T(8,128)(2,1)S(1)}, bf16[768,256]{1,0:T(8,1...) custom-call(bf16[16,256,128]{2,1,0:T(8,128)(2,1)} %refs_0_.1, ...), custom_call_target="tpu_custom_call" | custom-call | flops 2000000000 | bytes 8000000 | tf_op jit(solution)/shard_map/prepare/pallas_call | solution.py:260
  8.7 0.0 collective-permute-done.2.rec3
  8.7 0.4 collective-permute-done.1.rec2
  9.1 0.7 %collective-permute-done.rec1 = bf16[128,256]{1,0:T(8,128)(2,1)S(1)} collective-permute-done((bf16[128,256]{1,0:T(8,128)(2,1)S(1)}, bf16[128,256]{1,0:T(8,128)(2,1)S(1)}, u32[]{:S(2)}, u32[]{:S(2)}) %collective-permute-start) | collective-permute-done | bytes 65568 | tf_op jit(solution)/shard_map/ppermute | solution.py:258
  9.8 0.0 copy-done
  9.8 0.0 copy-done.1
  9.8 9.9 %synthesize.1 = bf16[512,256]{1,0:T(8,128)(2,1)S(1)} custom-call(bf16[512,256]{1,0:T(8,128)(2,1)S(1)} %bitcast.21, bf16[128,256]{1,0:T(8,128)(2,1)S(1)} %collective-permute-done.rec1, bf16[128,256]{1,0:T(8,128)(2,1)S(1)} %collective-permute-done.1.rec2, bf16[128,256]{1,0:T(8,128)(2,1)S(1)} %collective-permute-done.2.rec3, ...), custom_call_target="tpu_custom_call" | custom-call | flops 8000000000 | bytes 20000000 | tf_op jit(solution)/shard_map/synthesize/pallas_call | solution.py:303
  19.7 19.0 %all_to_all.11 = bf16[32,16,256]{2,1,0:T(8,128)(2,1)S(1)} all-to-all(bf16[32,16,256]{2,1,0:T(8,128)(2,1)S(1)} %bitcast.19), channel_id=1, replica_groups=mesh['section'=4,'group'=32] {'group'}, dimensions={0} | all-to-all | bytes 524288 | tf_op jit(solution)/shard_map/all_to_all | solution.py:326
  38.7 0.9 %place.1 = f32[512,128]{1,0:T(8,128)} custom-call(bf16[256,512]{1,0:T(8,128)(2,1)S(1)} %get-tuple-element.15.plac, bf16[512,256]{1,0:T(8,128)(2,1)S(1)} %bitcast.18), custom_call_target="tpu_custom_call" | custom-call | tf_op jit(solution)/shard_map/place/pallas_call | solution.py:327
Async XLA Ops:
  0.0 9.8 %copy-start = (bf16[64,8,256]{2,1,0:T(8,128)(2,1)S(1)}, bf16[64,8,256]{2,1,0:T(8,128)(2,1)}, u32[]{:S(2)}) copy-start(bf16[64,8,256]{2,1,0:T(8,128)(2,1)} %param.14) | copy-start | bytes 786436
  0.0 9.8 %copy-start.1 = (bf16[7,1024,512]{2,1,0:T(8,128)(2,1)S(1)}, bf16[7,1024,512]{2,1,0:T(8,128)(2,1)}, u32[]{:S(2)}) copy-start(bf16[7,1024,512]{2,1,0:T(8,128)(2,1)} %pre.1) | copy-start | bytes 22020100
  1.1 7.6 %collective-permute-start.2 = (bf16[128,256]{1,0:T(8,128)(2,1)S(1)}, bf16[128,256]{1,0:T(8,128)(2,1)S(1)}, u32[]{:S(2)}, u32[]{:S(2)}) collective-permute-start(bf16[128,256]{1,0:T(8,128)(2,1)S(1)} %get-tuple-element.25), channel_id=1, source_target_pairs={{0,96},{32,0},{64,32},{96,64},{1,97},{33,1},{65,33},{97,65},{2,98}... | collective-permute-start | bytes 196616 | tf_op jit(solution)/shard_map/ppermute | solution.py:258
  4.5 4.7 %collective-permute-start.1 = (bf16[128,256]{1,0:T(8,128)(2,1)S(1)}, bf16[128,256]{1,0:T(8,128)(2,1)S(1)}, u32[]{:S(2)}, u32[]{:S(2)}) collective-permute-start(bf16[128,256]{1,0:T(8,128)(2,1)S(1)} %get-tuple-element.26), channel_id=1, source_target_pairs={{0,64},{32,96},{64,0},{96,32},{1,65},{33,97},{65,1},{97,33},{2,66}... | collective-permute-start | bytes 196616 | tf_op jit(solution)/shard_map/ppermute | solution.py:258
  5.0 4.8 %collective-permute-start = (bf16[128,256]{1,0:T(8,128)(2,1)S(1)}, bf16[128,256]{1,0:T(8,128)(2,1)S(1)}, u32[]{:S(2)}, u32[]{:S(2)}) collective-permute-start(bf16[128,256]{1,0:T(8,128)(2,1)S(1)} %get-tuple-element.27), channel_id=1, source_target_pairs={{0,32},{32,64},{64,96},{96,0},{1,33},{33,65},{65,97},{97,1},{2,34}... | collective-permute-start | bytes 196616 | tf_op jit(solution)/shard_map/ppermute | solution.py:258

commit v2 on v1

--- a/solution.py
+++ b/solution.py
@@ -75,14 +75,11 @@
     copies = [pltpu.make_async_copy(a, b, sems.at[i]) for i, (a, b) in enumerate(zip(sources, (*held, up1)))]
     for copy in copies:
         copy.start()
-    for copy in copies[:11]:
-        copy.wait()
-    up2, up3, res3, up4, res4, post, owners, slot, start, lead, tail = held
+    post, up3, res3, up4, res4, owners, slot, start, lead, tail, up2 = held
     section = lax.axis_index("section")
     lane = lax.axis_index("group")
-    for j in range(8):
-        w2p[j, :, 0:128] = up2[2 * j]
-        w2p[j, :, 128:256] = up2[2 * j + 1]
+    for copy in copies[:10]:
+        copy.wait()
     b3[...] = blocks(spread_t(up3, 64), 128, 64, up_entries((0, 1, 2, -1), 4))
     r3[...] = blocks(
         spread(res3[...].reshape(192, 64), 64), 64, 64, res_entries((*range(4), *range(-4, 0), *range(4, 8)), 4)
@@ -101,15 +98,18 @@
         [dot(post_t, as_bf((tap == a + 6 - off) & (tap < 7))) for a in range(8)], axis=0
     ).astype(BF)
     off, smp = iota((128, 256), 0), iota((128, 256), 1)
-    for i in range(34):
-        wc[i] = dot(base, as_bf((smp == 8 * (i - 1) - 3 + off) & (off < 14))).astype(BF)
+    for i in range(9):
+        first = jnp.where(smp < 128, 8 * (i - 1) - 3, 128 + 8 * (i + 8) - 3)
+        both = dot(base, as_bf((smp == first + off) & (off < 14)))
+        wc[i] = both[:, 0:128].astype(BF)
+        wc[i + 9] = both[:, 128:256].astype(BF)
     owner = jnp.concatenate([owners[:, i * 128 : (i + 1) * 128] for i in range(16)], axis=0)
     mine = jnp.where(iota((16, 128), 0) == lane // 2, 1, 0)
     spot = lane % 2 * 64 + section * CD
     rowsel = lambda v: jnp.sum(v * mine, axis=0, keepdims=True).astype(F32)
-    pick = iota((128, 128), 1) == spot + iota((128, 128), 0) % CD
+    pick = iota((256, 128), 1) == spot + iota((256, 128), 0) % CD
     column = lambda v: jnp.sum(jnp.where(pick, rowsel(v), 0.0), axis=1, keepdims=True)
-    owner_col = column(owner)
+    owner_col = column(owner)[0:128]
     owner_row = jnp.sum(
         jnp.where(iota((128, 128), 0) == iota((128, 128), 1), owner_col, 0.0), axis=0, keepdims=True
     )
@@ -118,7 +118,7 @@
     dest = (2.0 * owner_row + rank).astype(jnp.int32)
     r_d, l_d = iota((512, 128), 0), iota((512, 128), 1)
     disp[...] = as_bf((r_d // FR == dest) & (r_d % FR == l_d // CD))
-    t = ((iota((128, 256), 0) // CD) * HOP + iota((128, 256), 1)).astype(F32) + 0.5
+    t = ((iota((256, 128), 0) // CD) * 128 + iota((256, 128), 1)).astype(F32) + 0.5
     win[...] = jnp.minimum(1.0, t / (HOP * column(lead[...]))) * jnp.minimum(
         1.0, (FR * HOP - t) / (HOP * column(tail[...]))
     )
@@ -138,6 +138,10 @@
     item = jnp.where(l_p // 32 == iota((16, 512), 0), item, 0.0)
     goal = jnp.sum(item, axis=0, keepdims=True).astype(jnp.int32) + iota((1, 512), 1) % FR
     plac[...] = as_bf(iota((256, 512), 0) == goal)
+    copies[10].wait()
+    for j in range(8):
+        w2p[j, :, 0:128] = up2[2 * j]
+        w2p[j, :, 128:256] = up2[2 * j + 1]
     copies[11].wait()
 
 
@@ -151,7 +155,7 @@
 
 
 def synthesize(
-    hid, rec1, rec2, rec3, pre, up1, w2p, b3, r3, b4, r4, wc, disp, win, out,
+    own, rec1, rec2, rec3, pre, up1, w2p, b3, r3, b4, r4, wc, disp, win, out,
     xb, a0, a1, a2, u3, i3, a3, u4, i4, a4,
 ):
     section = lax.axis_index("section")
@@ -163,8 +167,7 @@
 
     r, c = iota((128, 128), 0), iota((128, 128), 1)
     turn = as_bf(c == (r % CD) * FR + r // CD)
-    own = hid[pl.ds(pl.multiple_of(section * 128, 128), 128), :]
-    for d, block in enumerate((own, rec1[...], rec2[...], rec3[...])):
+    for d, block in enumerate((own[...], rec1[...], rec2[...], rec3[...])):
         xb[3 * CD : 3 * CD + 128, d * 256 : (d + 1) * 256] = dot(turn, block).astype(BF)
     acc = jnp.zeros((128, 512), F32)
     for d in range(SECT):
@@ -227,12 +230,28 @@
                 hi = ROWS if n == chunks - 1 else (n + 1) * CHUNK - behind * CD
                 stages[behind](lo, hi)
 
-    acc = jnp.zeros((128, 256), F32)
-    for i in range(34):
-        rows = [a4[fr * 512 + i * CD : fr * 512 + (i + 1) * CD, :] for fr in range(FR)]
-        acc = acc + dot(jnp.concatenate(rows, axis=0), wc[i])
+    near = [
+        jnp.concatenate([a4[(16 * half + i) * CD : (16 * half + i + 1) * CD, :] for half in range(2 * FR)], axis=0)
+        for i in range(18)
+    ]
+    acc = dot(jnp.concatenate(near, axis=1), wc[...].reshape(18 * 256, 128))
     wave = (jnp.tanh(acc) * win[...]).astype(BF)
-    out[...] = dot(disp[...], wave).astype(BF)
+    halves = [
+        jnp.concatenate([wave[(2 * fr + h) * CD : (2 * fr + h + 1) * CD] for fr in range(FR)], axis=0)
+        for h in range(2)
+    ]
+    out[...] = dot(disp[...], jnp.concatenate(halves, axis=1)).astype(BF)
+
+
+def cut(hid, own, to1, to2, to3, sems):
+    section = lax.axis_index("section")
+    copies = []
+    for d, block in ((1, to1), (2, to2), (3, to3), (0, own)):
+        rows = pl.ds(pl.multiple_of(lax.rem(section + d, SECT) * 128, 128), 128)
+        copies.append(pltpu.make_async_copy(hid.at[rows, :], block, sems.at[d]))
+        copies[-1].start()
+    for copy in copies:
+        copy.wait()
 
 
 def place(plac, rec, out):
@@ -250,13 +269,20 @@
     hidden, pre_weight, up1_weight, up2_weight, up3_weight, res3_weight, up4_weight, res4_weight,
     post_weight, owner_device, stream_slot, start_frame, lead_frames, tail_frames,
 ):
-    section = lax.axis_index("section")
-    rows_here = hidden.reshape(SECT, 128, 256)
-    received = []
-    for d in (1, 2, 3):
-        block = lax.dynamic_index_in_dim(rows_here, (section + d) % SECT, 0, keepdims=False)
-        received.append(lax.ppermute(block, "section", [(i, (i + d) % SECT) for i in range(SECT)]))
     shape = jax.ShapeDtypeStruct
+    own, *outgoing = pl.pallas_call(
+        cut,
+        out_shape=(shape((128, 256), BF),) * 4,
+        in_specs=[HB],
+        out_specs=(VM,) * 4,
+        scratch_shapes=[pltpu.SemaphoreType.DMA((SECT,))],
+        compiler_params=pltpu.CompilerParams(vmem_limit_bytes=4 * 1024 * 1024),
+        name="cut",
+    )(pltpu.with_memory_space_constraint(hidden.reshape(512, 256), pltpu.HBM))
+    received = [
+        lax.ppermute(block, "section", [(i, (i + d) % SECT) for i in range(SECT)])
+        for d, block in zip((1, 2, 3), outgoing)
+    ]
     prepared = pl.pallas_call(
         prepare,
         out_shape=(
@@ -266,22 +292,22 @@
             shape((768, 256), BF),
             shape((512, 256), BF),
             shape((512, 256), BF),
-            shape((34, 256, 256), BF),
+            shape((18, 256, 128), BF),
             shape((512, 128), BF),
             shape((256, 512), BF),
-            shape((128, 256), F32),
+            shape((256, 128), F32),
         ),
         in_specs=[HB] * 12,
         out_specs=(VM,) * 10,
         scratch_shapes=[
-            pltpu.VMEM((16, 256, 128), BF),
+            pltpu.VMEM((7, 32), BF),
             pltpu.VMEM((4, 64, 128), BF),
             pltpu.VMEM((3, 64, 64), BF),
             pltpu.VMEM((4, 32, 64), BF),
             pltpu.VMEM((3, 32, 32), BF),
-            pltpu.VMEM((7, 32), BF),
             pltpu.VMEM((1, 2048), jnp.int32),
             *[pltpu.VMEM((16, 128), jnp.int32)] * 4,
+            pltpu.VMEM((16, 256, 128), BF),
             pltpu.VMEM((128, 128), F32),
             pltpu.SemaphoreType.DMA((12,)),
         ],
@@ -292,9 +318,10 @@
         *(
             pltpu.with_memory_space_constraint(v, pltpu.HBM)
             for v in (
-                up2_weight, jnp.swapaxes(up3_weight, 1, 2), res3_weight, jnp.swapaxes(up4_weight, 1, 2),
-                res4_weight, post_weight, owner_device.reshape(1, 2048),
+                post_weight, jnp.swapaxes(up3_weight, 1, 2), res3_weight, jnp.swapaxes(up4_weight, 1, 2),
+                res4_weight, owner_device.reshape(1, 2048),
                 *(v.reshape(16, 128) for v in (stream_slot, start_frame, lead_frames, tail_frames)),
+                up2_weight,
                 up1_weight,
             )
         )
@@ -322,7 +349,7 @@
             flops=8_000_000_000, bytes_accessed=20_000_000, transcendentals=32768
         ),
         name="synthesize",
-    )(hidden.reshape(512, 256), *received, pre_weight, up1, w2p, b3, r3, b4, r4, wc, disp, win)
+    )(own, *received, pre_weight, up1, w2p, b3, r3, b4, r4, wc, disp, win)
     waves = lax.all_to_all(sent, "group", split_axis=0, concat_axis=0, tiled=True)
     streams = pl.pallas_call(
         place,

time: 39.7 us -> 38.5 us (0.970)
  starting transfers between devices: 4.5 us -> 5.71 us
  local copies, waits for them, and re-layouts: 1.07 us -> 0.01 us
  waiting for transfers between devices: 1.05 us -> 0.01 us
  blocking collectives: 19 us -> 18.4 us
    ppermute x3, starting transfers between devices: 4.5 us -> 5.71 us  [shards(): lax.ppermute(block, 'section', [(i, (i + d) % SECT) for i in range(SECT)])]
    pallas_call x0 -> x1, Pallas kernels: none -> 1.12 us  [shards(): pl.pallas_call(cut, out_shape=(shape((128, 256), BF),) * 4, in_specs=[HB]...]
    squeeze x1 -> x0, local copies, waits for them, and re-layouts: 1.07 us -> none  [shards(): lax.dynamic_index_in_dim(rows_here, (section + d) % SECT, 0, keepdims=False)]
    ppermute x3, waiting for transfers between devices: 1.05 us -> 0.01 us  [shards(): lax.ppermute(block, 'section', [(i, (i + d) % SECT) for i in range(SECT)])]
    all_to_all x1, blocking collectives: 19 us -> 18.4 us  [shards(): lax.all_to_all(sent, 'group', split_axis=0, concat_axis=0, tiled=True)]
    pallas_call x1, Pallas kernels: 9.89 us -> 9.4 us  [shards(): pl.pallas_call(synthesize, out_shape=shape((512, 256), BF), in_specs=[VM]...]
  transfers between devices with their start and end apart: 3 -> 3, of which waited for: 2 -> 0; matrix products, arithmetic and copies ran while one was open for 0% -> 0% of each run, Pallas kernels for 8% -> 7%
where the time goes in v2:
time: 38.5 us; the launch traced here: 38.4 us
  blocking collectives  18.4 us (48%)
  Pallas kernels  14.2 us (37%)
  starting transfers between devices  5.71 us (15%)
    all_to_all x1, blocking collectives, shards(): lax.all_to_all(sent, 'group', split_axis=0, concat_axis=0, tiled=True)  18.4 us
    pallas_call x1, Pallas kernels, shards(): pl.pallas_call(synthesize, out_shape=shape((512, 256), BF), in_specs=[VM]...  9.4 us
    ppermute x3, starting transfers between devices, shards(): lax.ppermute(block, 'section', [(i, (i + d) % SECT) for i in range(SECT)])  5.71 us
    pallas_call x1, Pallas kernels, shards(): pl.pallas_call(prepare, out_shape=(shape((16, 512, 256), BF), shape((8, 2...  2.79 us
    pallas_call x1, Pallas kernels, shards(): pl.pallas_call(cut, out_shape=(shape((128, 256), BF),) * 4, in_specs=[HB]...  1.12 us
    pallas_call x1, Pallas kernels, shards(): pl.pallas_call(place, out_shape=shape((512, 128), F32), in_specs=[VM] * 2...  0.94 us
  transfers between devices with their start and end apart: 3, of which 0 were waited for; matrix products, arithmetic and copies ran while one was open for 0% of the time, Pallas kernels for 7%

profile of v2, /device:TPU:1, one launch (start us, length us, event | category | flops | bytes accessed | tf_op | source)
XLA Modules:
  0.0 38.4 jit_solution(6134434452119583218)
XLA Ops:
  0.0 0.0 copy-start
  0.0 1.1 %cut.1 = (bf16[128,256]{1,0:T(8,128)(2,1)S(1)}, bf16[128,256]{1,0:T(8,128)(2,1)S(1)}, bf16[128,256]{1,0:T(8,128)(2,1)S(1)}, bf16[128,256]{1,0:T(8,128)(2,1)S(1)}) custom-call(bf16[512,256]{1,0:T(8,128)(2,1)} %bitcast.13), custom_call_target="tpu_custom_call" | custom-call | tf_op jit(solution)/shard_map/cut/pallas_call | solution.py:273
  1.1 2.1 %collective-permute-start = (bf16[128,256]{1,0:T(8,128)(2,1)S(1)}, bf16[128,256]{1,0:T(8,128)(2,1)S(1)}, u32[]{:S(2)}, u32[]{:S(2)}) collective-permute-start(bf16[128,256]{1,0:T(8,128)(2,1)S(1)} %get-tuple-element.21), channel_id=1, source_target_pairs={{0,32},{32,64},{64,96},{96,0},{1,33},{33,65},{65,97},{97,1},{2,34}... | collective-permute-start | bytes 196616 | tf_op jit(solution)/shard_map/ppermute | solution.py:283
  3.2 2.5 %collective-permute-start.1 = (bf16[128,256]{1,0:T(8,128)(2,1)S(1)}, bf16[128,256]{1,0:T(8,128)(2,1)S(1)}, u32[]{:S(2)}, u32[]{:S(2)}) collective-permute-start(bf16[128,256]{1,0:T(8,128)(2,1)S(1)} %get-tuple-element.22), channel_id=1, source_target_pairs={{0,64},{32,96},{64,0},{96,32},{1,65},{33,97},{65,1},{97,33},{2,66}... | collective-permute-start | bytes 196616 | tf_op jit(solution)/shard_map/ppermute | solution.py:283
  5.7 1.2 %collective-permute-start.2 = (bf16[128,256]{1,0:T(8,128)(2,1)S(1)}, bf16[128,256]{1,0:T(8,128)(2,1)S(1)}, u32[]{:S(2)}, u32[]{:S(2)}) collective-permute-start(bf16[128,256]{1,0:T(8,128)(2,1)S(1)} %get-tuple-element.23), channel_id=1, source_target_pairs={{0,96},{32,0},{64,32},{96,64},{1,97},{33,1},{65,33},{97,65},{2,98}... | collective-permute-start | bytes 196616 | tf_op jit(solution)/shard_map/ppermute | solution.py:283
  6.8 2.8 %prepare.1 = (bf16[16,512,256]{2,1,0:T(8,128)(2,1)S(1)}, bf16[8,256,256]{2,1,0:T(8,128)(2,1)S(1)}, bf16[512,256]{1,0:T(8,128)(2,1)S(1)}, bf16[768,256]{1,0:T(8,1...) custom-call(bf16[7,32]{1,0:T(8,128)(2,1)} %refs_0_.1, ...), custom_call_target="tpu_custom_call" | custom-call | flops 2000000000 | bytes 8000000 | tf_op jit(solution)/shard_map/prepare/pallas_call | solution.py:286
  9.6 0.0 collective-permute-done.rec1
  9.6 0.0 collective-permute-done.1.rec2
  9.7 0.0 collective-permute-done.2.rec3
  9.7 0.0 copy-done
  9.7 9.4 %synthesize.1 = bf16[512,256]{1,0:T(8,128)(2,1)S(1)} custom-call(bf16[128,256]{1,0:T(8,128)(2,1)S(1)} %get-tuple-element.20.own, bf16[128,256]{1,0:T(8,128)(2,1)S(1)} %collective-permute-done.rec1, bf16[128,256]{1,0:T(8,128)(2,1)S(1)} %collective-permute-done.1.rec2, bf16[128,256]{1,0:T(8,128)(2,1)S(1)} %collective-permute-done.2.rec3, ...), custom_call_target="tpu_custom_call" | custom-call | flops 8000000000 | bytes 20000000 | tf_op jit(solution)/shard_map/synthesize/pallas_call | solution.py:330
  19.1 18.4 %all_to_all.11 = bf16[32,16,256]{2,1,0:T(8,128)(2,1)S(1)} all-to-all(bf16[32,16,256]{2,1,0:T(8,128)(2,1)S(1)} %bitcast.12), channel_id=1, replica_groups=mesh['section'=4,'group'=32] {'group'}, dimensions={0} | all-to-all | bytes 524288 | tf_op jit(solution)/shard_map/all_to_all | solution.py:353
  37.5 0.9 %place.1 = f32[512,128]{1,0:T(8,128)} custom-call(bf16[256,512]{1,0:T(8,128)(2,1)S(1)} %get-tuple-element.19.plac, bf16[512,256]{1,0:T(8,128)(2,1)S(1)} %bitcast.11), custom_call_target="tpu_custom_call" | custom-call | tf_op jit(solution)/shard_map/place/pallas_call | solution.py:354
Async XLA Ops:
  0.0 9.7 %copy-start = (bf16[7,1024,512]{2,1,0:T(8,128)(2,1)S(1)}, bf16[7,1024,512]{2,1,0:T(8,128)(2,1)}, u32[]{:S(2)}) copy-start(bf16[7,1024,512]{2,1,0:T(8,128)(2,1)} %pre.1) | copy-start | bytes 22020100
  1.1 8.5 %collective-permute-start = (bf16[128,256]{1,0:T(8,128)(2,1)S(1)}, bf16[128,256]{1,0:T(8,128)(2,1)S(1)}, u32[]{:S(2)}, u32[]{:S(2)}) collective-permute-start(bf16[128,256]{1,0:T(8,128)(2,1)S(1)} %get-tuple-element.21), channel_id=1, source_target_pairs={{0,32},{32,64},{64,96},{96,0},{1,33},{33,65},{65,97},{97,1},{2,34}... | collective-permute-start | bytes 196616 | tf_op jit(solution)/shard_map/ppermute | solution.py:283
  3.2 6.4 %collective-permute-start.1 = (bf16[128,256]{1,0:T(8,128)(2,1)S(1)}, bf16[128,256]{1,0:T(8,128)(2,1)S(1)}, u32[]{:S(2)}, u32[]{:S(2)}) collective-permute-start(bf16[128,256]{1,0:T(8,128)(2,1)S(1)} %get-tuple-element.22), channel_id=1, source_target_pairs={{0,64},{32,96},{64,0},{96,32},{1,65},{33,97},{65,1},{97,33},{2,66}... | collective-permute-start | bytes 196616 | tf_op jit(solution)/shard_map/ppermute | solution.py:283
  5.7 4.0 %collective-permute-start.2 = (bf16[128,256]{1,0:T(8,128)(2,1)S(1)}, bf16[128,256]{1,0:T(8,128)(2,1)S(1)}, u32[]{:S(2)}, u32[]{:S(2)}) collective-permute-start(bf16[128,256]{1,0:T(8,128)(2,1)S(1)} %get-tuple-element.23), channel_id=1, source_target_pairs={{0,96},{32,0},{64,32},{96,64},{1,97},{33,1},{65,33},{97,65},{2,98}... | collective-permute-start | bytes 196616 | tf_op jit(solution)/shard_map/ppermute | solution.py:283

commit v3 on v2

--- a/solution.py
+++ b/solution.py
@@ -69,16 +69,32 @@
     ]
 
 
+def turn():
+    r, c = iota((128, 128), 0), iota((128, 128), 1)
+    return as_bf(c == (r % CD) * FR + r // CD)
+
+
+def taps_of(ref, first):
+    taps = [ref[j * CD : j * CD + 128, first : first + 256] for j in range(7)]
+    return jnp.concatenate(taps, axis=1)
+
+
 def prepare(*refs):
-    sources, (up1, w2p, b3, r3, b4, r4, wc, disp, plac, win), held = refs[:12], refs[12:22], refs[22:33]
-    scr, sems = refs[33:]
-    copies = [pltpu.make_async_copy(a, b, sems.at[i]) for i, (a, b) in enumerate(zip(sources, (*held, up1)))]
+    (own, pre), sources, (part, b3, r3, b4, r4, wc, disp, plac, win) = refs[:2], refs[2:12], refs[12:21]
+    held, (scr, xb, sems) = refs[21:31], refs[31:]
+    copies = [pltpu.make_async_copy(a, b, sems.at[i]) for i, (a, b) in enumerate(zip(sources, held))]
     for copy in copies:
         copy.start()
-    post, up3, res3, up4, res4, owners, slot, start, lead, tail, up2 = held
+    post, up3, res3, up4, res4, owners, slot, start, lead, tail = held
     section = lax.axis_index("section")
     lane = lax.axis_index("group")
-    for copy in copies[:10]:
+    zero = jnp.zeros((3 * CD, 256), BF)
+    xb[0 : 3 * CD, :] = zero
+    xb[3 * CD + 128 :, :] = zero
+    xb[3 * CD : 3 * CD + 128, :] = dot(turn(), own[...]).astype(BF)
+    rows = pl.ds(pl.multiple_of(section * 256, 256), 256)
+    part[...] = dot(taps_of(xb, 0), pre[:, rows, :].reshape(7 * 256, 512))
+    for copy in copies:
         copy.wait()
     b3[...] = blocks(spread_t(up3, 64), 128, 64, up_entries((0, 1, 2, -1), 4))
     r3[...] = blocks(
@@ -138,11 +154,6 @@
     item = jnp.where(l_p // 32 == iota((16, 512), 0), item, 0.0)
     goal = jnp.sum(item, axis=0, keepdims=True).astype(jnp.int32) + iota((1, 512), 1) % FR
     plac[...] = as_bf(iota((256, 512), 0) == goal)
-    copies[10].wait()
-    for j in range(8):
-        w2p[j, :, 0:128] = up2[2 * j]
-        w2p[j, :, 128:256] = up2[2 * j + 1]
-    copies[11].wait()
 
 
 def edges(ref, first, rows):
@@ -155,7 +166,7 @@
 
 
 def synthesize(
-    own, rec1, rec2, rec3, pre, up1, w2p, b3, r3, b4, r4, wc, disp, win, out,
+    part, rec1, rec2, rec3, pre, up1, up2, b3, r3, b4, r4, wc, disp, win, out,
     xb, a0, a1, a2, u3, i3, a3, u4, i4, a4,
 ):
     section = lax.axis_index("section")
@@ -165,15 +176,13 @@
         ref[0 : pad * CD, :] = zero
         ref[ref.shape[0] - pad * CD :, :] = zero
 
-    r, c = iota((128, 128), 0), iota((128, 128), 1)
-    turn = as_bf(c == (r % CD) * FR + r // CD)
-    for d, block in enumerate((own[...], rec1[...], rec2[...], rec3[...])):
-        xb[3 * CD : 3 * CD + 128, d * 256 : (d + 1) * 256] = dot(turn, block).astype(BF)
-    acc = jnp.zeros((128, 512), F32)
-    for d in range(SECT):
-        rows = pl.ds(pl.multiple_of(lax.rem(section + SECT - d, SECT) * 256, 256), 256)
-        for j in range(7):
-            acc = acc + dot(xb[j * CD : j * CD + 128, d * 256 : (d + 1) * 256], pre[j, rows, :])
+    flip = turn()
+    acc = part[...]
+    for d, block in enumerate((rec1, rec2, rec3)):
+        xb[3 * CD : 3 * CD + 128, d * 256 : (d + 1) * 256] = dot(flip, block[...]).astype(BF)
+    for d in range(3):
+        rows = pl.ds(pl.multiple_of(lax.rem(section + 3 - d, SECT) * 256, 256), 256)
+        acc = acc + dot(taps_of(xb, d * 256), pre[:, rows, :].reshape(7 * 256, 512))
     a0[CD : CD + 128, :] = leaky(acc, 0.1).astype(BF)
 
     for p in range(8):
@@ -191,7 +200,11 @@
         later = a1[first + 2 * CD : first + 2 * CD + 256, :]
         for q in range(4):
             side, j = (earlier, q + 6) if q < 2 else (later, q - 2)
-            y = leaky(dot(here, w2p[q + 2]) + dot(side, w2p[j]), 0.1).astype(BF)
+            taps = [
+                jnp.concatenate([up2[2 * k], up2[2 * k + 1]], axis=1) for k in (q + 2, j)
+            ]
+            pair = jnp.concatenate([here, side], axis=1)
+            y = leaky(dot(pair, jnp.concatenate(taps, axis=0)), 0.1).astype(BF)
             for i in range(16):
                 at = (4 * (part * 16 + i) + q + 1) * CD
                 a2[at : at + CD, :] = y[i * CD : (i + 1) * CD]
@@ -262,7 +275,7 @@
 
 VM = pl.BlockSpec(memory_space=pltpu.VMEM)
 HB = pl.BlockSpec(memory_space=pltpu.HBM)
-LIMIT = 33 * 1024 * 1024
+LIMIT = 24 * 1024 * 1024
 
 
 def shards(
@@ -277,6 +290,7 @@
         out_specs=(VM,) * 4,
         scratch_shapes=[pltpu.SemaphoreType.DMA((SECT,))],
         compiler_params=pltpu.CompilerParams(vmem_limit_bytes=4 * 1024 * 1024),
+        cost_estimate=pl.CostEstimate(flops=60_000_000_000, bytes_accessed=500_000, transcendentals=0),
         name="cut",
     )(pltpu.with_memory_space_constraint(hidden.reshape(512, 256), pltpu.HBM))
     received = [
@@ -286,8 +300,7 @@
     prepared = pl.pallas_call(
         prepare,
         out_shape=(
-            shape((16, 512, 256), BF),
-            shape((8, 256, 256), BF),
+            shape((128, 512), F32),
             shape((512, 256), BF),
             shape((768, 256), BF),
             shape((512, 256), BF),
@@ -297,8 +310,8 @@
             shape((256, 512), BF),
             shape((256, 128), F32),
         ),
-        in_specs=[HB] * 12,
-        out_specs=(VM,) * 10,
+        in_specs=[VM] * 2 + [HB] * 10,
+        out_specs=(VM,) * 9,
         scratch_shapes=[
             pltpu.VMEM((7, 32), BF),
             pltpu.VMEM((4, 64, 128), BF),
@@ -307,33 +320,33 @@
             pltpu.VMEM((3, 32, 32), BF),
             pltpu.VMEM((1, 2048), jnp.int32),
             *[pltpu.VMEM((16, 128), jnp.int32)] * 4,
-            pltpu.VMEM((16, 256, 128), BF),
             pltpu.VMEM((128, 128), F32),
-            pltpu.SemaphoreType.DMA((12,)),
+            pltpu.VMEM((128 + 6 * CD, 256), BF),
+            pltpu.SemaphoreType.DMA((10,)),
         ],
-        compiler_params=pltpu.CompilerParams(vmem_limit_bytes=14 * 1024 * 1024),
-        cost_estimate=pl.CostEstimate(flops=2_000_000_000, bytes_accessed=8_000_000, transcendentals=0),
+        compiler_params=pltpu.CompilerParams(vmem_limit_bytes=6 * 1024 * 1024),
+        cost_estimate=pl.CostEstimate(flops=1000000000, bytes_accessed=4000000, transcendentals=0),
         name="prepare",
     )(
+        own,
+        pre_weight,
         *(
             pltpu.with_memory_space_constraint(v, pltpu.HBM)
             for v in (
                 post_weight, jnp.swapaxes(up3_weight, 1, 2), res3_weight, jnp.swapaxes(up4_weight, 1, 2),
                 res4_weight, owner_device.reshape(1, 2048),
                 *(v.reshape(16, 128) for v in (stream_slot, start_frame, lead_frames, tail_frames)),
-                up2_weight,
-                up1_weight,
             )
         )
     )
-    up1, w2p, b3, r3, b4, r4, wc, disp, plac, win = prepared
+    part, b3, r3, b4, r4, wc, disp, plac, win = prepared
     sent = pl.pallas_call(
         synthesize,
         out_shape=shape((512, 256), BF),
         in_specs=[VM] * 14,
         out_specs=VM,
         scratch_shapes=[
-            pltpu.VMEM((128 + 6 * CD, 1024), BF),
+            pltpu.VMEM((128 + 6 * CD, 768), BF),
             pltpu.VMEM((128 + 2 * CD, 512), BF),
             pltpu.VMEM((1024 + 2 * CD, 256), BF),
             pltpu.VMEM((ROWS + 2 * CD, 256), BF),
@@ -349,7 +362,7 @@
             flops=8_000_000_000, bytes_accessed=20_000_000, transcendentals=32768
         ),
         name="synthesize",
-    )(own, *received, pre_weight, up1, w2p, b3, r3, b4, r4, wc, disp, win)
+    )(part, *received, pre_weight, up1_weight, up2_weight, b3, r3, b4, r4, wc, disp, win)
     waves = lax.all_to_all(sent, "group", split_axis=0, concat_axis=0, tiled=True)
     streams = pl.pallas_call(
         place,

time: 38.5 us -> 38.4 us (level)
  Pallas kernels: 14.2 us -> 13.4 us
  blocking collectives: 18.4 us -> 18.8 us
    pallas_call x1, Pallas kernels: 2.79 us -> 2.26 us  [shards(): pl.pallas_call(prepare, out_shape=(shape((128, 512), F32), shape((512, 25...]
    all_to_all x1, blocking collectives: 18.4 us -> 18.8 us  [shards(): lax.all_to_all(sent, 'group', split_axis=0, concat_axis=0, tiled=True)]
  transfers between devices with their start and end apart: 3 -> 3, of which waited for: 0 -> 1; matrix products, arithmetic and copies ran while one was open for 0% -> 0% of each run, Pallas kernels for 7% -> 6%
where the time goes in v3:
time: 38.4 us; the launch traced here: 38.2 us
  blocking collectives  18.8 us (49%)
  Pallas kernels  13.4 us (35%)
  starting transfers between devices  5.71 us (15%)
    all_to_all x1, blocking collectives, shards(): lax.all_to_all(sent, 'group', split_axis=0, concat_axis=0, tiled=True)  18.8 us
    pallas_call x1, Pallas kernels, shards(): pl.pallas_call(synthesize, out_shape=shape((512, 256), BF), in_specs=[VM]...  9.11 us
    ppermute x3, starting transfers between devices, shards(): lax.ppermute(block, 'section', [(i, (i + d) % SECT) for i in range(SECT)])  5.71 us
    pallas_call x1, Pallas kernels, shards(): pl.pallas_call(prepare, out_shape=(shape((128, 512), F32), shape((512, 25...  2.26 us
    pallas_call x1, Pallas kernels, shards(): pl.pallas_call(cut, out_shape=(shape((128, 256), BF),) * 4, in_specs=[HB]...  1.12 us
    pallas_call x1, Pallas kernels, shards(): pl.pallas_call(place, out_shape=shape((512, 128), F32), in_specs=[VM] * 2...  0.94 us
  transfers between devices with their start and end apart: 3, of which 1 were waited for; matrix products, arithmetic and copies ran while one was open for 0% of the time, Pallas kernels for 6%

profile of v3, /device:TPU:1, one launch (start us, length us, event | category | flops | bytes accessed | tf_op | source)
XLA Modules:
  0.0 38.2 jit_solution(13271513237882837890)
XLA Ops:
  0.0 0.0 copy-start
  0.0 1.1 %cut.1 = (bf16[128,256]{1,0:T(8,128)(2,1)S(1)}, bf16[128,256]{1,0:T(8,128)(2,1)S(1)}, bf16[128,256]{1,0:T(8,128)(2,1)S(1)}, bf16[128,256]{1,0:T(8,128)(2,1)S(1)}) custom-call(bf16[512,256]{1,0:T(8,128)(2,1)} %bitcast.20), custom_call_target="tpu_custom_call" | custom-call | flops 60000002048 | bytes 500000 | tf_op jit(solution)/shard_map/cut/pallas_call | solution.py:286
  1.1 0.0 copy-start.1
  1.1 0.0 copy-start.2
  1.2 2.1 %collective-permute-start = (bf16[128,256]{1,0:T(8,128)(2,1)S(1)}, bf16[128,256]{1,0:T(8,128)(2,1)S(1)}, u32[]{:S(2)}, u32[]{:S(2)}) collective-permute-start(bf16[128,256]{1,0:T(8,128)(2,1)S(1)} %get-tuple-element.21), channel_id=1, source_target_pairs={{0,32},{32,64},{64,96},{96,0},{1,33},{33,65},{65,97},{97,1},{2,34}... | collective-permute-start | bytes 196616 | tf_op jit(solution)/shard_map/ppermute | solution.py:297
  3.3 2.5 %collective-permute-start.1 = (bf16[128,256]{1,0:T(8,128)(2,1)S(1)}, bf16[128,256]{1,0:T(8,128)(2,1)S(1)}, u32[]{:S(2)}, u32[]{:S(2)}) collective-permute-start(bf16[128,256]{1,0:T(8,128)(2,1)S(1)} %get-tuple-element.22), channel_id=1, source_target_pairs={{0,64},{32,96},{64,0},{96,32},{1,65},{33,97},{65,1},{97,33},{2,66}... | collective-permute-start | bytes 196616 | tf_op jit(solution)/shard_map/ppermute | solution.py:297
  5.7 1.2 %collective-permute-start.2 = (bf16[128,256]{1,0:T(8,128)(2,1)S(1)}, bf16[128,256]{1,0:T(8,128)(2,1)S(1)}, u32[]{:S(2)}, u32[]{:S(2)}) collective-permute-start(bf16[128,256]{1,0:T(8,128)(2,1)S(1)} %get-tuple-element.23), channel_id=1, source_target_pairs={{0,96},{32,0},{64,32},{96,64},{1,97},{33,1},{65,33},{97,65},{2,98}... | collective-permute-start | bytes 196616 | tf_op jit(solution)/shard_map/ppermute | solution.py:297
  6.9 0.0 copy-done
  6.9 2.3 %prepare.1 = (f32[128,512]{1,0:T(8,128)S(1)}, bf16[512,256]{1,0:T(8,128)(2,1)S(1)}, bf16[768,256]{1,0:T(8,128)(2,1)S(1)}, bf16[512,256]{1,0:T(8,128)(2,1)S(1)}, ...) custom-call(bf16[128,256]{1,0:T(8,128)(2,1)S(1)} %get-tuple-element., ...), custom_call_target="tpu_custom_call" | custom-call | flops 1000000000 | bytes 4000000 | tf_op jit(solution)/shard_map/prepare/pallas_call | solution.py:300
  9.1 0.0 collective-permute-done.rec1
  9.1 0.0 collective-permute-done.1.rec2
  9.2 0.1 collective-permute-done.2.rec3
  9.3 0.0 copy-done.1
  9.3 0.0 copy-done.2
  9.3 9.1 %synthesize.1 = bf16[512,256]{1,0:T(8,128)(2,1)S(1)} custom-call(f32[128,512]{1,0:T(8,128)S(1)} %get-tuple-element.20.part, bf16[128,256]{1,0:T(8,128)(2,1)S(1)} %collective-permute-done.rec1, bf16[128,256]{1,0:T(8,128)(2,1)S(1)} %collective-permute-done.1.rec2, bf16[128,256]{1,0:T(8,128)(2,1)S(1)} %collective-permute-done.2.rec3, ...), custom_call_target="tpu_custom_call" | custom-call | flops 8000000000 | bytes 20000000 | tf_op jit(solution)/shard_map/synthesize/pallas_call | solution.py:343
  18.4 18.8 %all_to_all.11 = bf16[32,16,256]{2,1,0:T(8,128)(2,1)S(1)} all-to-all(bf16[32,16,256]{2,1,0:T(8,128)(2,1)S(1)} %bitcast.12), channel_id=1, replica_groups=mesh['section'=4,'group'=32] {'group'}, dimensions={0} | all-to-all | bytes 524288 | tf_op jit(solution)/shard_map/all_to_all | solution.py:366
  37.2 0.9 %place.1 = f32[512,128]{1,0:T(8,128)} custom-call(bf16[256,512]{1,0:T(8,128)(2,1)S(1)} %get-tuple-element.19.plac, bf16[512,256]{1,0:T(8,128)(2,1)S(1)} %bitcast.11), custom_call_target="tpu_custom_call" | custom-call | tf_op jit(solution)/shard_map/place/pallas_call | solution.py:367
Async XLA Ops:
  0.0 6.9 %copy-start = (bf16[7,1024,512]{2,1,0:T(8,128)(2,1)S(1)}, bf16[7,1024,512]{2,1,0:T(8,128)(2,1)}, u32[]{:S(2)}) copy-start(bf16[7,1024,512]{2,1,0:T(8,128)(2,1)} %pre.1) | copy-start | bytes 22020100
  1.1 8.2 %copy-start.1 = (bf16[16,512,256]{2,1,0:T(8,128)(2,1)S(1)}, bf16[16,512,256]{2,1,0:T(8,128)(2,1)}, u32[]{:S(2)}) copy-start(bf16[16,512,256]{2,1,0:T(8,128)(2,1)} %up1.1) | copy-start | bytes 12582916
  1.1 8.1 %copy-start.2 = (bf16[16,256,128]{2,1,0:T(8,128)(2,1)S(1)}, bf16[16,256,128]{2,1,0:T(8,128)(2,1)}, u32[]{:S(2)}) copy-start(bf16[16,256,128]{2,1,0:T(8,128)(2,1)} %up2.1) | copy-start | bytes 3145732
  1.2 8.0 %collective-permute-start = (bf16[128,256]{1,0:T(8,128)(2,1)S(1)}, bf16[128,256]{1,0:T(8,128)(2,1)S(1)}, u32[]{:S(2)}, u32[]{:S(2)}) collective-permute-start(bf16[128,256]{1,0:T(8,128)(2,1)S(1)} %get-tuple-element.21), channel_id=1, source_target_pairs={{0,32},{32,64},{64,96},{96,0},{1,33},{33,65},{65,97},{97,1},{2,34}... | collective-permute-start | bytes 196616 | tf_op jit(solution)/shard_map/ppermute | solution.py:297
  3.3 5.9 %collective-permute-start.1 = (bf16[128,256]{1,0:T(8,128)(2,1)S(1)}, bf16[128,256]{1,0:T(8,128)(2,1)S(1)}, u32[]{:S(2)}, u32[]{:S(2)}) collective-permute-start(bf16[128,256]{1,0:T(8,128)(2,1)S(1)} %get-tuple-element.22), channel_id=1, source_target_pairs={{0,64},{32,96},{64,0},{96,32},{1,65},{33,97},{65,1},{97,33},{2,66}... | collective-permute-start | bytes 196616 | tf_op jit(solution)/shard_map/ppermute | solution.py:297
  5.7 3.6 %collective-permute-start.2 = (bf16[128,256]{1,0:T(8,128)(2,1)S(1)}, bf16[128,256]{1,0:T(8,128)(2,1)S(1)}, u32[]{:S(2)}, u32[]{:S(2)}) collective-permute-start(bf16[128,256]{1,0:T(8,128)(2,1)S(1)} %get-tuple-element.23), channel_id=1, source_target_pairs={{0,96},{32,0},{64,32},{96,64},{1,97},{33,1},{65,33},{97,65},{2,98}... | collective-permute-start | bytes 196616 | tf_op jit(solution)/shard_map/ppermute | solution.py:297

commit v4 on v3

--- a/solution.py
+++ b/solution.py
@@ -166,7 +166,7 @@
 
 
 def synthesize(
-    part, rec1, rec2, rec3, pre, up1, up2, b3, r3, b4, r4, wc, disp, win, out,
+    part, rec2, rec3, rec1, pre, up1, up2, b3, r3, b4, r4, wc, disp, win, out,
     xb, a0, a1, a2, u3, i3, a3, u4, i4, a4,
 ):
     section = lax.axis_index("section")
@@ -181,7 +181,7 @@
     for d, block in enumerate((rec1, rec2, rec3)):
         xb[3 * CD : 3 * CD + 128, d * 256 : (d + 1) * 256] = dot(flip, block[...]).astype(BF)
     for d in range(3):
-        rows = pl.ds(pl.multiple_of(lax.rem(section + 3 - d, SECT) * 256, 256), 256)
+        rows = pl.ds(pl.multiple_of((section ^ (d + 1)) * 256, 256), 256)
         acc = acc + dot(taps_of(xb, d * 256), pre[:, rows, :].reshape(7 * 256, 512))
     a0[CD : CD + 128, :] = leaky(acc, 0.1).astype(BF)
 
@@ -260,7 +260,7 @@
     section = lax.axis_index("section")
     copies = []
     for d, block in ((1, to1), (2, to2), (3, to3), (0, own)):
-        rows = pl.ds(pl.multiple_of(lax.rem(section + d, SECT) * 128, 128), 128)
+        rows = pl.ds(pl.multiple_of((section ^ d) * 128, 128), 128)
         copies.append(pltpu.make_async_copy(hid.at[rows, :], block, sems.at[d]))
         copies[-1].start()
     for copy in copies:
@@ -294,8 +294,8 @@
         name="cut",
     )(pltpu.with_memory_space_constraint(hidden.reshape(512, 256), pltpu.HBM))
     received = [
-        lax.ppermute(block, "section", [(i, (i + d) % SECT) for i in range(SECT)])
-        for d, block in zip((1, 2, 3), outgoing)
+        lax.ppermute(block, "section", [(i, i ^ d) for i in range(SECT)])
+        for d, block in zip((2, 3, 1), (outgoing[1], outgoing[2], outgoing[0]))
     ]
     prepared = pl.pallas_call(
         prepare,

time: 38.4 us -> 38.4 us (level)
  starting transfers between devices: 5.71 us -> 4.52 us
  waiting for transfers between devices: 0.13 us -> 1.18 us
    ppermute x3, starting transfers between devices: 5.71 us -> 4.52 us  [shards(): lax.ppermute(block, 'section', [(i, i ^ d) for i in range(SECT)])]
    ppermute x3, waiting for transfers between devices: 0.13 us -> 1.18 us  [shards(): lax.ppermute(block, 'section', [(i, i ^ d) for i in range(SECT)])]
where the time goes in v4:
time: 38.4 us; the launch traced here: 38.2 us
  blocking collectives  19 us (49%)
  Pallas kernels  13.4 us (35%)
  starting transfers between devices  4.52 us (12%)
  waiting for transfers between devices  1.18 us (3%)
    all_to_all x1, blocking collectives, shards(): lax.all_to_all(sent, 'group', split_axis=0, concat_axis=0, tiled=True)  19 us
    pallas_call x1, Pallas kernels, shards(): pl.pallas_call(synthesize, out_shape=shape((512, 256), BF), in_specs=[VM]...  9.1 us
    ppermute x3, starting transfers between devices, shards(): lax.ppermute(block, 'section', [(i, i ^ d) for i in range(SECT)])  4.52 us
    pallas_call x1, Pallas kernels, shards(): pl.pallas_call(prepare, out_shape=(shape((128, 512), F32), shape((512, 25...  2.26 us
    ppermute x3, waiting for transfers between devices, shards(): lax.ppermute(block, 'section', [(i, i ^ d) for i in range(SECT)])  1.18 us
    pallas_call x1, Pallas kernels, shards(): pl.pallas_call(cut, out_shape=(shape((128, 256), BF),) * 4, in_specs=[HB]...  1.12 us
    pallas_call x1, Pallas kernels, shards(): pl.pallas_call(place, out_shape=shape((512, 128), F32), in_specs=[VM] * 2...  0.94 us
  transfers between devices with their start and end apart: 3, of which 1 were waited for; matrix products, arithmetic and copies ran while one was open for 0% of the time, Pallas kernels for 6%

profile of v4, /device:TPU:1, one launch (start us, length us, event | category | flops | bytes accessed | tf_op | source)
XLA Modules:
  0.0 38.2 jit_solution(11957779397563066944)
XLA Ops:
  0.0 0.0 copy-start
  0.0 1.1 %cut.1 = (bf16[128,256]{1,0:T(8,128)(2,1)S(1)}, bf16[128,256]{1,0:T(8,128)(2,1)S(1)}, bf16[128,256]{1,0:T(8,128)(2,1)S(1)}, bf16[128,256]{1,0:T(8,128)(2,1)S(1)}) custom-call(bf16[512,256]{1,0:T(8,128)(2,1)} %bitcast.20), custom_call_target="tpu_custom_call" | custom-call | flops 60000002048 | bytes 500000 | tf_op jit(solution)/shard_map/cut/pallas_call | solution.py:286
  1.1 0.0 copy-start.1
  1.1 0.0 copy-start.2
  1.2 3.7 %collective-permute-start = (bf16[128,256]{1,0:T(8,128)(2,1)S(1)}, bf16[128,256]{1,0:T(8,128)(2,1)S(1)}, u32[]{:S(2)}, u32[]{:S(2)}) collective-permute-start(bf16[128,256]{1,0:T(8,128)(2,1)S(1)} %get-tuple-element.21), channel_id=1, source_target_pairs={{0,64},{32,96},{64,0},{96,32},{1,65},{33,97},{65,1},{97,33},{2,66}... | collective-permute-start | bytes 196616 | tf_op jit(solution)/shard_map/ppermute | solution.py:297
  4.8 0.9 %collective-permute-start.1 = (bf16[128,256]{1,0:T(8,128)(2,1)S(1)}, bf16[128,256]{1,0:T(8,128)(2,1)S(1)}, u32[]{:S(2)}, u32[]{:S(2)}) collective-permute-start(bf16[128,256]{1,0:T(8,128)(2,1)S(1)} %get-tuple-element.22), channel_id=1, source_target_pairs={{0,96},{32,64},{64,32},{96,0},{1,97},{33,65},{65,33},{97,1},{2,98}... | collective-permute-start | bytes 196616 | tf_op jit(solution)/shard_map/ppermute | solution.py:297
  5.7 0.0 collective-permute-start.2
  5.7 0.0 copy-done
  5.7 2.3 %prepare.1 = (f32[128,512]{1,0:T(8,128)S(1)}, bf16[512,256]{1,0:T(8,128)(2,1)S(1)}, bf16[768,256]{1,0:T(8,128)(2,1)S(1)}, bf16[512,256]{1,0:T(8,128)(2,1)S(1)}, ...) custom-call(bf16[128,256]{1,0:T(8,128)(2,1)S(1)} %get-tuple-element., ...), custom_call_target="tpu_custom_call" | custom-call | flops 1000000000 | bytes 4000000 | tf_op jit(solution)/shard_map/prepare/pallas_call | solution.py:300
  7.9 0.0 collective-permute-done.rec2
  8.0 1.2 %collective-permute-done.1.rec3 = bf16[128,256]{1,0:T(8,128)(2,1)S(1)} collective-permute-done((bf16[128,256]{1,0:T(8,128)(2,1)S(1)}, bf16[128,256]{1,0:T(8,128)(2,1)S(1)}, u32[]{:S(2)}, u32[]{:S(2)}) %collective-permute-start.1) | collective-permute-done | bytes 65568 | tf_op jit(solution)/shard_map/ppermute | solution.py:297
  9.1 0.0 collective-permute-done.2.rec1
  9.1 0.0 copy-done.1
  9.1 0.0 copy-done.2
  9.1 9.1 %synthesize.1 = bf16[512,256]{1,0:T(8,128)(2,1)S(1)} custom-call(f32[128,512]{1,0:T(8,128)S(1)} %get-tuple-element.20.part, bf16[128,256]{1,0:T(8,128)(2,1)S(1)} %collective-permute-done.rec2, bf16[128,256]{1,0:T(8,128)(2,1)S(1)} %collective-permute-done.1.rec3, bf16[128,256]{1,0:T(8,128)(2,1)S(1)} %collective-permute-done.2.rec1, ...), custom_call_target="tpu_custom_call" | custom-call | flops 8000000000 | bytes 20000000 | tf_op jit(solution)/shard_map/synthesize/pallas_call | solution.py:343
  18.2 19.0 %all_to_all.11 = bf16[32,16,256]{2,1,0:T(8,128)(2,1)S(1)} all-to-all(bf16[32,16,256]{2,1,0:T(8,128)(2,1)S(1)} %bitcast.12), channel_id=1, replica_groups=mesh['section'=4,'group'=32] {'group'}, dimensions={0} | all-to-all | bytes 524288 | tf_op jit(solution)/shard_map/all_to_all | solution.py:366
  37.2 0.9 %place.1 = f32[512,128]{1,0:T(8,128)} custom-call(bf16[256,512]{1,0:T(8,128)(2,1)S(1)} %get-tuple-element.19.plac, bf16[512,256]{1,0:T(8,128)(2,1)S(1)} %bitcast.11), custom_call_target="tpu_custom_call" | custom-call | tf_op jit(solution)/shard_map/place/pallas_call | solution.py:367
Async XLA Ops:
  0.0 5.7 %copy-start = (bf16[7,1024,512]{2,1,0:T(8,128)(2,1)S(1)}, bf16[7,1024,512]{2,1,0:T(8,128)(2,1)}, u32[]{:S(2)}) copy-start(bf16[7,1024,512]{2,1,0:T(8,128)(2,1)} %pre.1) | copy-start | bytes 22020100
  1.1 8.0 %copy-start.1 = (bf16[16,512,256]{2,1,0:T(8,128)(2,1)S(1)}, bf16[16,512,256]{2,1,0:T(8,128)(2,1)}, u32[]{:S(2)}) copy-start(bf16[16,512,256]{2,1,0:T(8,128)(2,1)} %up1.1) | copy-start | bytes 12582916
  1.1 8.0 %copy-start.2 = (bf16[16,256,128]{2,1,0:T(8,128)(2,1)S(1)}, bf16[16,256,128]{2,1,0:T(8,128)(2,1)}, u32[]{:S(2)}) copy-start(bf16[16,256,128]{2,1,0:T(8,128)(2,1)} %up2.1) | copy-start | bytes 3145732
  1.2 6.8 %collective-permute-start = (bf16[128,256]{1,0:T(8,128)(2,1)S(1)}, bf16[128,256]{1,0:T(8,128)(2,1)S(1)}, u32[]{:S(2)}, u32[]{:S(2)}) collective-permute-start(bf16[128,256]{1,0:T(8,128)(2,1)S(1)} %get-tuple-element.21), channel_id=1, source_target_pairs={{0,64},{32,96},{64,0},{96,32},{1,65},{33,97},{65,1},{97,33},{2,66}... | collective-permute-start | bytes 196616 | tf_op jit(solution)/shard_map/ppermute | solution.py:297
  4.8 4.3 %collective-permute-start.1 = (bf16[128,256]{1,0:T(8,128)(2,1)S(1)}, bf16[128,256]{1,0:T(8,128)(2,1)S(1)}, u32[]{:S(2)}, u32[]{:S(2)}) collective-permute-start(bf16[128,256]{1,0:T(8,128)(2,1)S(1)} %get-tuple-element.22), channel_id=1, source_target_pairs={{0,96},{32,64},{64,32},{96,0},{1,97},{33,65},{65,33},{97,1},{2,98}... | collective-permute-start | bytes 196616 | tf_op jit(solution)/shard_map/ppermute | solution.py:297
  5.7 3.5 %collective-permute-start.2 = (bf16[128,256]{1,0:T(8,128)(2,1)S(1)}, bf16[128,256]{1,0:T(8,128)(2,1)S(1)}, u32[]{:S(2)}, u32[]{:S(2)}) collective-permute-start(bf16[128,256]{1,0:T(8,128)(2,1)S(1)} %get-tuple-element.23), channel_id=1, source_target_pairs={{0,32},{32,0},{64,96},{96,64},{1,33},{33,1},{65,97},{97,65},{2,34}... | collective-permute-start | bytes 196616 | tf_op jit(solution)/shard_map/ppermute | solution.py:297
